TPU v7x, 32 devices: a whole 2x2x4 slice. The times are simulated.
32 devices in a mesh: gz: 8 (over z, x), gy: 2 (over core), gx: 2 (over y).
Axes of the slice: x: 2, y: 2, z: 4, core: 2. Of those that a mesh axis runs over, the one named last changes fastest.
Arguments:
- grid_input: bfloat16 [64, 32, 4096], P('gz', 'gy', 'gx'), may hold values from -6 to 6
- pre_one: bfloat16 [64, 32, 4096], P('gz', 'gy', 'gx'), may hold values from -5.875 to 4.125
- pre_two: bfloat16 [64, 32, 4096], P('gz', 'gy', 'gx'), may hold values from -8 to 8
- grad_output: bfloat16 [64, 32, 4096], P('gz', 'gy', 'gx'), may hold values from -6 to 6
- spectral_one: bfloat16 [16, 16, 16, 4096], P('gz', 'gy', 'gx'), may hold values from -1.5 to 1.5
- spectral_two: bfloat16 [16, 16, 16, 4096], P('gz', 'gy', 'gx'), may hold values from -1.5 to 1.5
- point_one: bfloat16 [64, 64], replicated, may hold values from -0.75 to 0.75
- point_two: bfloat16 [64, 64], replicated, may hold values from -0.75 to 0.75
Outputs:
- input_grad: bfloat16 [64, 32, 4096], P('gz', 'gy', 'gx')
- spectral_grad_one: float32 [16, 16, 16, 4096], P('gz', 'gy', 'gx')
- spectral_grad_two: float32 [16, 16, 16, 4096], P('gz', 'gy', 'gx')
- point_grad_one: float32 [64, 64], replicated
- point_grad_two: float32 [64, 64], replicated
All inputs are finite; a program needn't handle non-finite values.
Results may differ from a plain program's by a relative error of at most 0.012.
Values sent between devices are 32-bit elements; how exact they have to be, the bound alone decides.
A program may use at most 64 MiB of HBM per device.

v0:
```python
import math

import jax
import jax.numpy as jnp
from jax import lax
from jax.sharding import PartitionSpec as P

MX = 16
MY = 16
MZ = 16


highest = lax.Precision.HIGHEST
inv_root_two = 0.7071067811865476
inv_root_tau = 0.3989422804014327


def frequency_list(mode_count, length):
    position = jnp.arange(mode_count, dtype=jnp.int32)
    return jnp.where(position < mode_count // 2, position, length - mode_count + position)


def local_positions(cell_count, device_count, device_index):
    return jnp.arange(cell_count, dtype=jnp.int32) * device_count + device_index


def cas_table(mode_count, length, positions):
    frequency = frequency_list(mode_count, length)
    product = frequency[:, None] * positions[None, :] % length
    phase = product.astype(jnp.float32) * (2.0 * math.pi / length)
    return (jnp.cos(phase) + jnp.sin(phase)).astype(jnp.bfloat16)


def gelu_value(pre_value):
    return pre_value * 0.5 * (1.0 + jax.scipy.special.erf(pre_value * inv_root_two))


def gelu_slope(pre_value):
    normal_cdf = 0.5 * (1.0 + jax.scipy.special.erf(pre_value * inv_root_two))
    return normal_cdf + pre_value * jnp.exp(-0.5 * pre_value * pre_value) * inv_root_tau


def to_modes(layer_in, pre_grad, tables):
    table_x, table_y, table_z = tables
    float_y = table_y.astype(jnp.float32)
    float_x = table_x.astype(jnp.float32)
    table_rows = table_z
    first = jnp.einsum("kz,xyzc->kxyc", table_rows, layer_in, preferred_element_type=jnp.float32)
    second = jnp.einsum("kz,xyzc->kxyc", table_rows, pre_grad, preferred_element_type=jnp.float32)
    section_z = lax.psum_scatter(
        jnp.stack((first, second), axis=1), "gx", scatter_dimension=0, tiled=True
    )
    table_rows = float_y
    section_y = lax.psum_scatter(
        jnp.einsum("ky,dnxyc->kdnxc", table_rows, section_z, precision=highest),
        "gy",
        scatter_dimension=0,
        tiled=True,
    )
    table_rows = float_x
    section_x = lax.psum_scatter(
        jnp.einsum("kx,bdnxc->kbdnc", table_rows, section_y, precision=highest),
        "gz",
        scatter_dimension=0,
        tiled=True,
    )
    return (section_x[:, :, :, 0, :], section_x[:, :, :, 1, :])


def from_modes(hat_back, tables):
    table_x, table_y, table_z = [t.astype(jnp.float32) for t in tables]
    table_rows = table_x
    part_x = jnp.einsum(
        "kx,kbdc->xbdc",
        table_rows,
        lax.all_gather(hat_back, "gz", axis=0, tiled=True),
        precision=highest,
    )
    table_rows = table_y
    part_y = jnp.einsum(
        "ky,xkdc->xydc",
        table_rows,
        lax.all_gather(part_x, "gy", axis=1, tiled=True),
        precision=highest,
    )
    table_rows = table_z
    return jnp.einsum(
        "kz,xykc->xyzc",
        table_rows,
        lax.all_gather(part_y, "gx", axis=2, tiled=True),
        precision=highest,
    )


def layer_back(layer_in, pre_act, upstream, spectral, point, tables, scales):
    analysis, synthesis = scales
    channels = point.shape[0]
    pre_grad = (upstream * gelu_slope(pre_act.astype(jnp.float32))).astype(jnp.bfloat16)
    hat_in, hat_grad = to_modes(layer_in, pre_grad, tables)
    hat_in = analysis * hat_in
    hat_grad = synthesis * hat_grad
    weights = spectral.reshape(hat_in.shape + (channels,)).astype(jnp.float32)
    spec_grad = (hat_in[..., :, None] * hat_grad[..., None, :]).reshape(spectral.shape)
    hat_back = jnp.einsum("ijkao,ijko->ijka", weights, hat_grad, precision=highest)
    flat_in = layer_in.reshape(-1, channels)
    flat_grad = pre_grad.reshape(-1, channels)
    point_term = jnp.einsum("ni,no->io", flat_in, flat_grad, preferred_element_type=jnp.float32)
    local_term = jnp.dot(flat_grad, point.T, preferred_element_type=jnp.float32).reshape(
        layer_in.shape
    )
    down = analysis * from_modes(hat_back, tables) + local_term
    return (down, spec_grad, point_term)


def point_total(point_term):
    return lax.psum(point_term, ("gz", "gy", "gx"))


def on_device(
    grid_input, pre_one, pre_two, grad_output, spectral_one, spectral_two, point_one, point_two
):
    channels = point_one.shape[0]
    size_x, size_y, size_z = (lax.axis_size("gz"), lax.axis_size("gy"), lax.axis_size("gx"))
    cells_x = grid_input.shape[0]
    cells_y = grid_input.shape[1]
    cells_z = grid_input.shape[2] // channels
    tables = (
        cas_table(MX, cells_x * size_x, local_positions(cells_x, size_x, lax.axis_index("gz"))),
        cas_table(MY, cells_y * size_y, local_positions(cells_y, size_y, lax.axis_index("gy"))),
        cas_table(MZ, cells_z * size_z, local_positions(cells_z, size_z, lax.axis_index("gx"))),
    )
    total_cells = cells_x * size_x * cells_y * size_y * cells_z * size_z
    total_modes = MX * MY * MZ
    cell_scale = total_cells ** (-0.5)
    scales = ((total_cells * total_modes) ** (-0.25), cell_scale)
    shape_local = (cells_x, cells_y, cells_z, channels)
    first_in = grid_input.reshape(shape_local)
    first_pre = pre_one.reshape(shape_local)
    second_pre = pre_two.reshape(shape_local)
    upstream = grad_output.reshape(shape_local).astype(jnp.float32)
    middle = gelu_value(first_pre.astype(jnp.float32)).astype(jnp.bfloat16)
    down_two, spec_two, term_two = layer_back(
        middle, second_pre, upstream, spectral_two, point_two, tables, scales
    )
    grad_two = point_total(term_two) * cell_scale
    down_one, spec_one, term_one = layer_back(
        first_in, first_pre, down_two, spectral_one, point_one, tables, scales
    )
    grad_one = point_total(term_one) * cell_scale
    input_grad = down_one.astype(jnp.bfloat16).reshape(cells_x, cells_y, cells_z * channels)
    return (input_grad, spec_one, spec_two, grad_one, grad_two)


def solution(mesh):
    in_specs = (
        P("gz", "gy", "gx"),
        P("gz", "gy", "gx"),
        P("gz", "gy", "gx"),
        P("gz", "gy", "gx"),
        P("gz", "gy", "gx", None),
        P("gz", "gy", "gx", None),
        P(),
        P(),
    )
    out_specs = (
        P("gz", "gy", "gx"),
        P("gz", "gy", "gx", None),
        P("gz", "gy", "gx", None),
        P(),
        P(),
    )
    return jax.shard_map(
        on_device, mesh=mesh, in_specs=in_specs, out_specs=out_specs, check_vma=False
    )
```

profile of v0, /device:TPU:0, one launch (start us, length us, event | category | flops | bytes accessed | tf_op | source)
XLA Modules:
  0.0 379.1 jit_solution(14758147522219332984)
XLA Ops:
  7.3 3.0 reshape.110
  10.3 2.3 reshape.111
  12.5 0.9 reshape.109
  13.5 2.6 fusion.5
  16.2 1.0 copy-done.1
  18.1 1.5 pad_maximum_fusion
  19.7 34.6 %reduce-scatter.7.cloned.1.call-done = f32[8,2,8,16,64]{4,0,3,2,1:T(8,128)} async-done(((f32[16,2,8,16,64]{4,0,3,2,1:T(8,128)}), f32[8,2,8,16,64]{4,0,3,2,1:T(8,128)}) %reduce-scatter.7.cloned.1.call-update) | async-done | bytes 524304 | tf_op jit(solution)/shard_map/reduce_scatter | solution.py:50
  54.3 3.0 fusion.25
  57.4 8.6 %reduce-scatter.9.cloned.1.call-done = f32[8,8,2,8,64]{4,0,3,2,1:T(8,128)} async-done(((f32[16,8,2,8,64]{4,0,3,2,1:T(8,128)}), f32[8,8,2,8,64]{4,0,3,2,1:T(8,128)}) %reduce-scatter.9.cloned.1.call-update) | async-done | bytes 262160 | tf_op jit(solution)/shard_map/reduce_scatter | solution.py:54
  66.0 1.8 fusion.36
  67.8 1.6 copy.47
  69.5 3.3 reshape.105
  72.7 2.1 reshape.104
  74.8 1.4 convolution_bitcast_fusion.3
  76.2 58.5 %reduce-scatter.11.cloned.1.call-done = f32[2,8,8,2,64]{4,2,3,1,0:T(8,128)} async-done(((f32[16,8,8,2,64]{4,2,3,1,0:T(8,128)}), f32[2,8,8,2,64]{4,2,3,1,0:T(8,128)}) %reduce-scatter.11.cloned.1.call-update) | async-done | bytes 65552 | tf_op jit(solution)/shard_map/reduce_scatter | solution.py:61
  134.7 0.9 fusion.38
  135.6 4.9 %fusion.143 = f32[2,8,8,1,64]{4,3,2,1,0:T(1,128)S(1)} fusion(f32[2,8,8,64,1]{3,4,2,1,0:T(1,128)S(1)} %bitcast.115, bf16[2,8,8,64,64]{4,3,2,1,0:T(8,128)(2,1)} %reshape.105), kind=kOutput, calls=%fused_computation.187 | convolution fusion | flops 6291456 | bytes 1114112 | tf_op jit(solution)/shard_map/ijkao,ijko->ijka/dot_general | solution.py:104
  140.5 31.5 %all_gather.18 = f32[16,8,8,64]{3,2,1,0:T(8,128)S(1)} all-gather(f32[2,8,8,64]{3,2,1,0:T(8,128)S(1)} %bitcast.116), channel_id=1, replica_groups=mesh['gz'=8,'gy'=2,'gx'=2] {'gz'}, dimensions={0}, use_global_device_ids=true | all-gather | bytes 294912 | tf_op jit(solution)/shard_map/all_gather | solution.py:76
  172.8 2.2 all_gather.19
  175.7 15.0 %all_gather.20 = f32[8,16,16,64]{3,1,2,0:T(8,128)S(1)} all-gather(f32[8,16,8,64]{3,1,2,0:T(8,128)S(1)} %convolution_bitcast_fusion.5), channel_id=1, replica_groups=mesh['gz'=8,'gy'=2,'gx'=2] {'gx'}, dimensions={2}, use_global_device_ids=true | all-gather | bytes 786432 | tf_op jit(solution)/shard_map/all_gather | solution.py:90
  190.6 1.3 fusion.23
  191.9 1.3 fusion.11
  194.5 1.5 pad_maximum_fusion.1
  196.0 1.0 copy-done.4
  197.0 1.1 reshape_reshape.3
  198.1 4.3 %reshape.106 = bf16[2,8,8,64,64]{4,3,2,1,0:T(8,128)(2,1)} reshape(bf16[2,8,8,4096]{3,2,1,0:T(8,128)(2,1)} %param.12) | data formatting | bytes 2097152 | tf_op jit(solution)/shard_map/reshape | solution.py:102
  202.3 24.4 %reduce-scatter.13.cloned.1.call-done = f32[8,2,8,16,64]{4,0,3,2,1:T(8,128)} async-done(((f32[16,2,8,16,64]{4,0,3,2,1:T(8,128)}), f32[8,2,8,16,64]{4,0,3,2,1:T(8,128)}) %reduce-scatter.13.cloned.1.call-update) | async-done | bytes 524304 | tf_op jit(solution)/shard_map/reduce_scatter | solution.py:50
  226.8 3.0 fusion.21
  229.9 1.0 multiply_convert_fusion.2
  230.9 2.1 convert_element_type.104
  232.9 2.5 fusion.18
  235.4 2.8 convert_element_type.108
  238.2 1.7 convolution_bitcast_fusion.6
  240.0 1.8 fusion.31
  241.8 1.6 copy.55
  243.4 2.6 broadcast_multiply_fusion
  246.0 4.8 %mul.314 = f32[2,8,8,4096]{3,2,1,0:T(8,128)} reshape(f32[2,8,8,64,64]{4,3,2,1,0:T(8,128)} %broadcast_multiply_fusion) | data formatting | bytes 4194304 | tf_op jit(solution)/shard_map/mul | solution.py:103
  251.2 40.3 %all-reduce = (f32[64,64]{0,1:T(8,128)S(1)}, f32[64,64]{0,1:T(8,128)S(1)}) all-reduce(f32[64,64]{0,1:T(8,128)S(1)} %convolution_bitcast_fusion.7, f32[64,64]{0,1:T(8,128)S(1)} %convolution_bitcast_fusion.6), channel_id=1, replica_groups=mesh['gz'=8,'gy'=2,'gx'=2] {'gz','gy','gx'}, use_global_device_ids=true, to_apply=%region_6.7 | all-reduce | flops 8192 | bytes 65536 | tf_op jit(solution)/shard_map/psum | solution.py:116
  292.9 14.5 %reduce-scatter.17.cloned.1.call-done = f32[2,8,8,2,64]{4,2,3,1,0:T(8,128)} async-done(((f32[16,8,8,2,64]{4,2,3,1,0:T(8,128)}), f32[2,8,8,2,64]{4,2,3,1,0:T(8,128)}) %reduce-scatter.17.cloned.1.call-update) | async-done | bytes 65552 | tf_op jit(solution)/shard_map/reduce_scatter | solution.py:61
  307.4 0.9 fusion.39
  308.3 2.6 broadcast_multiply_fusion.1
  310.9 4.9 %mul.308 = f32[2,8,8,4096]{3,2,1,0:T(8,128)} reshape(f32[2,8,8,64,64]{4,3,2,1,0:T(8,128)} %broadcast_multiply_fusion.1) | data formatting | bytes 4194304 | tf_op jit(solution)/shard_map/mul | solution.py:103
  315.8 3.3 fusion.144
  319.1 31.5 %all_gather.21 = f32[16,8,8,64]{3,2,1,0:T(8,128)S(1)} all-gather(f32[2,8,8,64]{3,2,1,0:T(8,128)S(1)} %bitcast.117), channel_id=1, replica_groups=mesh['gz'=8,'gy'=2,'gx'=2] {'gz'}, dimensions={0}, use_global_device_ids=true | all-gather | bytes 294912 | tf_op jit(solution)/shard_map/all_gather | solution.py:76
  351.4 2.2 all_gather.22
  354.3 14.6 %all_gather.23 = f32[8,16,16,64]{3,1,2,0:T(8,128)S(1)} all-gather(f32[8,16,8,64]{3,1,2,0:T(8,128)S(1)} %convolution_bitcast_fusion.4), channel_id=1, replica_groups=mesh['gz'=8,'gy'=2,'gx'=2] {'gx'}, dimensions={2}, use_global_device_ids=true | all-gather | bytes 786432 | tf_op jit(solution)/shard_map/all_gather | solution.py:90
  368.9 1.3 fusion.19
  370.7 1.6 reshape.107
  (52 shorter events, 7.8 us)
Async XLA Ops:
  7.2 184.8 %copy-start = (bf16[64,64]{1,0:T(8,128)(2,1)S(1)}, bf16[64,64]{1,0:T(8,128)(2,1)}, u32[]{:S(2)}) copy-start(bf16[64,64]{1,0:T(8,128)(2,1)} %param.15) | copy-start | bytes 24580
  7.2 3.1 copy-start.5
  7.2 47.1 %reduce-scatter.7.cloned.1.call-start = ((), (), s32[]{:S(2)}) async-start(), calls=%async_computation.6 | async-start | bytes 3145728 | tf_op jit(solution)/shard_map/reduce_scatter | solution.py:50
  7.3 5.3 %copy-start.6 = (bf16[8,16,2048]{2,1,0:T(8,128)(2,1)S(1)}, bf16[8,16,2048]{2,1,0:T(8,128)(2,1)}, u32[]{:S(2)}) copy-start(bf16[8,16,2048]{2,1,0:T(8,128)(2,1)} %param.9) | copy-start | bytes 1572868
  16.1 1.0 copy-start.1
  19.6 46.4 %reduce-scatter.9.cloned.1.call-start = ((), (), s32[]{:S(2)}) async-start(), calls=%async_computation.7 | async-start | bytes 1572864 | tf_op jit(solution)/shard_map/reduce_scatter | solution.py:54
  57.3 77.4 %reduce-scatter.11.cloned.1.call-start = ((), (), s32[]{:S(2)}) async-start(), calls=%async_computation.8 | async-start | bytes 1179648 | tf_op jit(solution)/shard_map/reduce_scatter | solution.py:61
  57.4 12.1 %copy-start.9 = (bf16[2,8,8,4096]{3,2,1,0:T(8,128)(2,1)S(1)}, bf16[2,8,8,4096]{3,2,1,0:T(8,128)(2,1)}, u32[]{:S(2)}) copy-start(bf16[2,8,8,4096]{3,2,1,0:T(8,128)(2,1)} %param.13) | copy-start | bytes 3145732
  69.4 157.4 %reduce-scatter.13.cloned.1.call-start = ((), (), s32[]{:S(2)}) async-start(), calls=%async_computation.9 | async-start | bytes 3145728 | tf_op jit(solution)/shard_map/reduce_scatter | solution.py:50
  175.7 16.3 %copy-start.2 = (bf16[8,16,32,64]{3,2,1,0:T(8,128)(2,1)S(1)}, bf16[8,16,32,64]{3,2,1,0:T(8,128)(2,1)}, u32[]{:S(2)}) copy-start(bf16[8,16,32,64]{3,2,1,0:T(8,128)(2,1)} %copy-done.1) | copy-start | bytes 1572868
  193.2 1.2 copy-start.3
  196.0 1.0 copy-start.4
  196.0 44.0 %reduce-scatter.15.cloned.1.call-start = ((), (), s32[]{:S(2)}) async-start(), calls=%async_computation.10 | async-start | bytes 1572864 | tf_op jit(solution)/shard_map/reduce_scatter | solution.py:54
  202.3 27.5 %copy-start.7 = (bf16[8,16,2048]{2,1,0:T(8,128)(2,1)S(1)}, bf16[8,16,2048]{2,1,0:T(8,128)(2,1)}, u32[]{:S(2)}) copy-start(bf16[8,16,2048]{2,1,0:T(8,128)(2,1)} %param.9) | copy-start | bytes 1572868
  229.8 77.6 %reduce-scatter.17.cloned.1.call-start = ((), (), s32[]{:S(2)}) async-start(), calls=%async_computation.11 | async-start | bytes 1179648 | tf_op jit(solution)/shard_map/reduce_scatter | solution.py:61
  310.9 4.9 %copy-start.8 = (bf16[2,8,8,64,64]{4,3,2,1,0:T(8,128)(2,1)S(1)}, bf16[2,8,8,64,64]{4,3,2,1,0:T(8,128)(2,1)}, u32[]{:S(2)}) copy-start(bf16[2,8,8,64,64]{4,3,2,1,0:T(8,128)(2,1)} %reshape.106) | copy-start | bytes 3145732
  354.3 15.9 %copy-start.10 = (bf16[64,64]{1,0:T(8,128)(2,1)S(1)}, bf16[64,64]{1,0:T(8,128)(2,1)}, u32[]{:S(2)}) copy-start(bf16[64,64]{1,0:T(8,128)(2,1)} %param.14) | copy-start | bytes 24580
Sparse Core Ops, SparseCore 0:
  19.7 34.5 reduce-scatter.6
  57.5 8.5 reduce-scatter.8
  70.0 64.6 reduce-scatter.10
  196.1 30.6 reduce-scatter.12
  229.9 8.5 reduce-scatter.14
  243.5 63.8 reduce-scatter.16
where the time goes:
time: 380 us; the launch traced here: 379 us
  waiting for transfers between devices  141 us (37%)
  blocking collectives  137 us (36%)
  local copies, waits for them, and re-layouts  40.4 us (11%)
  matrix products  29.8 us (8%)
  other arithmetic  16.1 us (4%)
  between operations  14.4 us (4%)
    reduce_scatter x2, waiting for transfers between devices, to_modes(): lax.psum_scatter(jnp.einsum('kx,bdnxc->kbdnc', table_rows, section_y, pre...  73 us
    all_gather x2, blocking collectives, from_modes(): lax.all_gather(hat_back, 'gz', axis=0, tiled=True)  63.1 us
    reduce_scatter x2, waiting for transfers between devices, to_modes(): lax.psum_scatter(jnp.stack((first, second), axis=1), 'gx', scatter_dimens...  59.1 us
    psum x1, blocking collectives, point_total(): return lax.psum(point_term, ('gz', 'gy', 'gx'))  40.3 us
    all_gather x2, blocking collectives, from_modes(): lax.all_gather(part_y, 'gx', axis=2, tiled=True)  29.6 us
    mul x2, local copies, waits for them, and re-layouts, layer_back(): hat_in[..., :, None] * hat_grad[..., None, :]  9.66 us
    reduce_scatter x2, waiting for transfers between devices, to_modes(): lax.psum_scatter(jnp.einsum('ky,dnxyc->kdnxc', table_rows, section_z, pre...  8.62 us
    dot_general x2, matrix products, layer_back(): jnp.einsum('ijkao,ijko->ijka', weights, hat_grad, precision=highest)  8.27 us
  transfers between devices with their start and end apart: 6, of which 5 were waited for; matrix products, arithmetic and copies ran while one was open for 8% of the time, Pallas kernels for 0%

commit v1 on v0

v1 whole, which is shorter than its diff:
```python
import functools
import math

import jax
import jax.numpy as jnp
import ml_dtypes
import numpy as np
from jax import lax
from jax.experimental import pallas as pl
from jax.experimental.pallas import tpu as pltpu
from jax.sharding import PartitionSpec as P

MX = 16
MY = 16
MZ = 16

inv_root_two = 0.7071067811865476
inv_root_tau = 0.3989422804014327
bf16 = jnp.bfloat16
f32 = jnp.float32


def cas_tables(mode_count, cells, devices):
    length = cells * devices
    mode = np.arange(mode_count)
    frequency = np.where(mode < mode_count // 2, mode, length - mode_count + mode)
    position = np.arange(cells)[None, :] * devices + np.arange(devices)[:, None]
    product = (frequency[None, :, None] * position[:, None, :]) % length
    phase = product.astype(np.float32) * np.float32(2.0 * math.pi / length)
    return (np.cos(phase) + np.sin(phase)).astype(ml_dtypes.bfloat16).astype(np.float32)


def const(values):
    return jnp.asarray(np.asarray(values).astype(ml_dtypes.bfloat16))


def gelu_both(pre_value):
    cdf = 0.5 * (1.0 + lax.erf(pre_value * inv_root_two))
    slope = cdf + pre_value * jnp.exp(-0.5 * pre_value * pre_value) * inv_root_tau
    return pre_value * cdf, slope


def mm(a, b):
    return jnp.dot(a.astype(bf16), b.astype(bf16), preferred_element_type=f32)


def mm_t(a, b):
    return lax.dot_general(
        a.astype(bf16), b.astype(bf16), (((1,), (1,)), ((), ())), preferred_element_type=f32
    )


def tmm(a, b):
    return lax.dot_general(
        a.astype(bf16), b.astype(bf16), (((0,), (0,)), ((), ())), preferred_element_type=f32
    )


def layer_kernel(cfg, *refs):
    nz, ny, nx = cfg["nz"], cfg["ny"], cfg["nx"]
    first = cfg["first"]
    brow, blane = cfg["brow"], cfg["blane"]
    mrow = cfg["mrow"]
    a_scale, b_scale = cfg["scales"]
    chan = cfg["chan"]
    n_a = ny * nx
    names = cfg["names"]
    r = dict(zip(names, refs))
    kz, ay, ax, axt, ayt = r["kz"], r["ay"], r["ax"], r["axt"], r["ayt"]
    gz, gy, gx = lax.axis_index("gz"), lax.axis_index("gy"), lax.axis_index("gx")

    def wrap(v, n):
        return lax.rem(v, n)

    def a_peer(j):
        return wrap(gy + j // nx, ny), wrap(gx + j % nx, nx)

    def a_device(j):
        py, px = a_peer(j)
        return (gz, py, px)

    def b_device(j):
        return (wrap(gz + j, nz), gy, gx)

    barrier = pltpu.get_barrier_semaphore()
    for j in range(1, n_a):
        pl.semaphore_signal(barrier, 1, device_id=a_device(j), device_id_type=pl.DeviceIdType.MESH)
    for j in range(1, nz):
        pl.semaphore_signal(barrier, 1, device_id=b_device(j), device_id_type=pl.DeviceIdType.MESH)

    width = kz.shape[1]
    tile = 256
    lanes = kz.shape[0]
    copies = []

    def remote(src, dst, sem, j, dev):
        c = pltpu.make_async_remote_copy(
            src_ref=src, dst_ref=dst, send_sem=r[sem + "_s"].at[j], recv_sem=r[sem + "_r"].at[j],
            device_id=dev, device_id_type=pl.DeviceIdType.MESH,
        )
        c.start()
        copies.append(c)
        return c

    def analyse(src, t):
        table_y = ay[gy]

        def body(n, carry):
            cols = pl.ds(pl.multiple_of(n * tile, tile), tile)
            part = mm(src[...], kz[:, cols])
            r["y"][t, :, cols] = mm(table_y, part)
            return carry

        lax.fori_loop(0, width // tile, body, 0)

    def block(py, px):
        return (
            pl.ds(pl.multiple_of(py * brow, brow), brow),
            pl.ds(pl.multiple_of(px * blane, blane), blane),
        )

    def start_a(t):
        out = []
        for j in range(1, n_a):
            rows, cols = block(*a_peer(j))
            out.append(
                remote(r["y"].at[t, rows, cols], r["land_a"].at[t, j], "a%d" % t, j, a_device(j))
            )
        return out

    def finish_a(t, cs):
        rows, cols = block(gy, gx)
        for c in cs:
            c.wait_recv()
        total = r["y"][t, rows, cols]
        for j in range(1, n_a):
            total = total + r["land_a"][t, j]
        part = mm(ax[gz], total)
        for s in range(nz):
            r["p"][t, s] = part[s * mrow : (s + 1) * mrow, :]
        out = []
        for j in range(1, nz):
            dev = b_device(j)
            out.append(remote(r["p"].at[t, dev[0]], r["land_b"].at[t, j], "b%d" % t, j, dev))
        return out

    def finish_b(t, cs, scale):
        for c in cs:
            c.wait_recv()
        total = r["p"][t, gz]
        for j in range(1, nz):
            total = total + r["land_b"][t, j]
        spread = mm(r["rep"][...], total * scale) * r["mask"][...]
        return mm(spread, r["fold"][...])

    analyse(r["dz"], 0)
    pl.semaphore_wait(barrier, n_a + nz - 2)
    wait_a = start_a(0)
    if first:
        lane = lax.broadcasted_iota(jnp.int32, (chan, 2 * chan), 1)

        def point_part(left, right):
            total = jnp.zeros((2 * chan, 2 * chan), f32)

            def body(n, acc):
                cols = pl.ds(pl.multiple_of(n * 2 * chan, 2 * chan), 2 * chan)
                return acc + tmm(left[:, cols], right[:, cols])

            return lax.fori_loop(0, lanes // (2 * chan), body, total)

        pa = point_part(r["mid"], r["dz_two"])
        pb = point_part(r["gin"], r["dz"])
        low = lane < chan
        keep = jnp.where(low, pa[:chan], pb[chan:])
        turn = jnp.where(low, pb[:chan], pa[chan:])
        r["pt_a"][gy * nx + gx] = keep + pltpu.roll(turn, chan, 1)
        wait_pa = [
            remote(
                r["pt_a"].at[gy * nx + gx], r["pt_a"].at[gy * nx + gx], "pa", j, a_device(j)
            )
            for j in range(1, n_a)
        ]
    else:
        analyse(r["mid"], 1)
        wait_a1 = start_a(1)
        analyse(r["gin"], 2)
        wait_a2 = start_a(2)
    wait_b = finish_a(0, wait_a)
    tall = mm_t(r["eye"][...], r["point"][...])
    square = mm_t(tall, r["eye"][...])
    row_i = lax.broadcasted_iota(jnp.int32, square.shape, 0) // chan
    col_i = lax.broadcasted_iota(jnp.int32, square.shape, 1) // chan
    r["p4"][...] = jnp.where(row_i == col_i, square, 0.0).astype(bf16)
    if first:
        for c in wait_pa:
            c.wait_recv()
        total = r["pt_a"][0]
        for j in range(1, n_a):
            total = total + r["pt_a"][j]
        r["pt_b"][gz] = total
        wait_pb = [
            remote(r["pt_b"].at[gz], r["pt_b"].at[gz], "pb", j, b_device(j))
            for j in range(1, nz)
        ]
    hat = finish_b(0, wait_b, b_scale)
    wide = r["weights"].shape[1]
    prod_tile = jnp.concatenate([hat] * (512 // hat.shape[1]), axis=1)
    back = jnp.zeros((hat.shape[0], chan), f32)
    for n in range(wide // 512):
        w = r["weights"][:, n * 512 : (n + 1) * 512].astype(f32)
        back = back + mm(w * prod_tile, r["sum_o"][n * 512 : (n + 1) * 512, :])
    spread = mm(back, r["spread"][...]) * r["mask"][...]
    r["c"][gz] = tmm(r["rep"][...], spread)
    wait_c = [
        remote(r["c"].at[gz], r["c"].at[gz], "c", j, b_device(j)) for j in range(1, nz)
    ]
    if not first:
        wait_b1 = finish_a(1, wait_a1)
        wait_b2 = finish_a(2, wait_a2)
    for c in wait_c:
        c.wait_recv()
    for s in range(nz):
        r["cat"][s * mrow : (s + 1) * mrow, :] = r["c"][s]
    rows, cols = block(gy, gx)
    r["v"][rows, cols] = mm(axt[gz], r["cat"][...])
    wait_d = [
        remote(r["v"].at[rows, cols], r["v"].at[rows, cols], "d", j, a_device(j))
        for j in range(1, n_a)
    ]
    if first:
        hat_in = r["hat_in"][...]
    else:
        hat_in = finish_b(1, wait_b1, a_scale)
        r["hat_out"][...] = finish_b(2, wait_b2, a_scale)
    low_in = hat_in[:, :chan]
    for n in range(wide // 512):
        cs = slice(n * 512, (n + 1) * 512)
        r["spec"][:, cs] = mm_t(low_in, r["sum_o"][cs, :]) * prod_tile
    if first:
        for c in wait_pb:
            c.wait_recv()
        total = r["pt_b"][0]
        for j in range(1, nz):
            total = total + r["pt_b"][j]
        r["pt"][...] = total * b_scale
    for c in wait_d:
        c.wait_recv()
    r["v2"][...] = (mm(ayt[gy], r["v"][...]) * a_scale).astype(bf16)

    def body(n, carry):
        cs = pl.ds(pl.multiple_of(n * tile, tile), tile)
        r["down"][:, cs] = (
            mm_t(r["v2"][...], kz[cs, :]) + mm(r["dz"][:, cs], r["p4"][...])
        ).astype(r["down"].dtype)
        return carry

    lax.fori_loop(0, lanes // tile, body, 0)
    for c in copies:
        c.wait_send()


def on_device(
    grid_input, pre_one, pre_two, grad_output, spectral_one, spectral_two, point_one, point_two
):
    chan = point_one.shape[0]
    nz, ny, nx = (lax.axis_size("gz"), lax.axis_size("gy"), lax.axis_size("gx"))
    cx, cy = grid_input.shape[:2]
    lanes = grid_input.shape[2]
    cz = lanes // chan
    qx, qy, qz = MX // nz, MY // ny, MZ // nx
    total_cells = cx * nz * cy * ny * cz * nx
    b_scale = total_cells ** (-0.5)
    a_scale = (total_cells * MX * MY * MZ) ** (-0.25)
    tx, ty, tz = cas_tables(MX, cx, nz), cas_tables(MY, cy, ny), cas_tables(MZ, cz, nx)
    eye = np.eye(chan, dtype=np.float32)
    kz_all = np.zeros((nx, cz, chan, MZ, chan), ml_dtypes.bfloat16)
    diag = np.arange(chan)
    kz_all[:, :, diag, :, diag] = tz.transpose(0, 2, 1).astype(ml_dtypes.bfloat16)[None]
    kz = lax.dynamic_index_in_dim(
        const(kz_all.reshape(nx, lanes, MZ * chan)), lax.axis_index("gx"), 0, False
    )
    ay = np.einsum("dky,xw->dkxwy", ty, np.eye(cx)).reshape(ny, MY * cx, cx * cy)
    ax = np.einsum("dkx,ab->dkabx", tx, np.eye(qy)).reshape(nz, MX * qy, qy * cx)
    modes = qx * qy * qz
    mrow = qx * qy
    blane = qz * chan
    mode = np.arange(modes)
    rep = (mode[:, None] // qz == np.arange(mrow)[None, :]).astype(np.float32)
    mask = (mode[:, None] % qz == np.arange(blane)[None, :] // chan).astype(np.float32)
    fold = np.tile(np.concatenate([eye, eye], axis=1), (qz, 1))
    spread = np.tile(eye, (1, qz))
    sum_o = np.repeat(eye, chan, axis=0)
    eye4 = np.tile(eye, (256 // chan, 1))
    tables = {
        "kz": kz,
        "ay": const(ay),
        "ax": const(ax),
        "axt": const(ax.transpose(0, 2, 1)),
        "ayt": const(ay.transpose(0, 2, 1)),
        "rep": const(rep),
        "mask": jnp.asarray(mask),
        "fold": const(fold),
        "spread": const(spread),
        "sum_o": const(sum_o),
        "eye": const(eye4),
    }
    rows = cx * cy
    brow = qy * cx
    n_a = ny * nx

    def call(first, ins):
        args = dict(ins, **tables)
        t = 1 if first else 3
        outs = {
            "down": jax.ShapeDtypeStruct((rows, lanes), bf16 if first else f32),
            "spec": jax.ShapeDtypeStruct((modes, chan * chan), f32),
        }
        if first:
            outs["pt"] = jax.ShapeDtypeStruct((chan, 2 * chan), f32)
        else:
            outs["hat_out"] = jax.ShapeDtypeStruct((modes, 2 * chan), f32)
        scratch = {
            "y": pltpu.VMEM((t, MY * cx, MZ * chan), f32),
            "land_a": pltpu.VMEM((t, n_a, brow, blane), f32),
            "p": pltpu.VMEM((t, nz, mrow, blane), f32),
            "land_b": pltpu.VMEM((t, nz, mrow, blane), f32),
            "c": pltpu.VMEM((nz, mrow, blane), f32),
            "cat": pltpu.VMEM((nz * mrow, blane), f32),
            "v": pltpu.VMEM((MY * cx, MZ * chan), f32),
            "v2": pltpu.VMEM((rows, MZ * chan), bf16),
            "p4": pltpu.VMEM((256, 256), bf16),
        }
        sems = {"c": nz, "d": n_a}
        for k in range(t):
            sems["a%d" % k] = n_a
            sems["b%d" % k] = nz
        if first:
            scratch["pt_a"] = pltpu.VMEM((n_a, chan, 2 * chan), f32)
            scratch["pt_b"] = pltpu.VMEM((nz, chan, 2 * chan), f32)
            sems["pa"] = n_a
            sems["pb"] = nz
        for k, n in sems.items():
            scratch[k + "_s"] = pltpu.SemaphoreType.DMA((n,))
            scratch[k + "_r"] = pltpu.SemaphoreType.DMA((n,))
        cfg = dict(
            nz=nz, ny=ny, nx=nx, first=first, brow=brow, blane=blane, mrow=mrow,
            scales=(a_scale, b_scale), chan=chan,
            names=list(args) + list(outs) + list(scratch),
        )
        vmem = pl.BlockSpec(memory_space=pltpu.VMEM)
        got = pl.pallas_call(
            functools.partial(layer_kernel, cfg),
            out_shape=list(outs.values()),
            in_specs=[vmem] * len(args),
            out_specs=[vmem] * len(outs),
            scratch_shapes=list(scratch.values()),
            compiler_params=pltpu.CompilerParams(
                collective_id=1 if first else 0,
                has_side_effects=True,
                vmem_limit_bytes=48 * 1024 * 1024,
            ),
            name="layer_one" if first else "layer_two",
        )(*args.values())
        return dict(zip(outs, got))

    flat = (rows, lanes)
    gin = grid_input.reshape(flat)
    value_one, slope_one = gelu_both(pre_one.reshape(flat).astype(f32))
    _, slope_two = gelu_both(pre_two.reshape(flat).astype(f32))
    mid = value_one.astype(bf16)
    dz_two = (grad_output.reshape(flat).astype(f32) * slope_two).astype(bf16)
    two = call(
        False,
        {
            "dz": dz_two,
            "mid": mid,
            "gin": gin,
            "weights": spectral_two.reshape(modes, chan * chan),
            "point": point_two,
        },
    )
    dz_one = (two["down"] * slope_one).astype(bf16)
    one = call(
        True,
        {
            "dz": dz_one,
            "mid": mid,
            "gin": gin,
            "dz_two": dz_two,
            "hat_in": two["hat_out"],
            "weights": spectral_one.reshape(modes, chan * chan),
            "point": point_one,
        },
    )
    return (
        one["down"].reshape(grid_input.shape),
        one["spec"].reshape(spectral_one.shape),
        two["spec"].reshape(spectral_two.shape),
        one["pt"][:, chan:],
        one["pt"][:, :chan],
    )


def solution(mesh):
    grid = P("gz", "gy", "gx")
    spec = P("gz", "gy", "gx", None)
    return jax.shard_map(
        on_device,
        mesh=mesh,
        in_specs=(grid, grid, grid, grid, spec, spec, P(), P()),
        out_specs=(grid, spec, spec, P(), P()),
        check_vma=False,
    )
```

time: 380 us -> 102 us (0.27)
  waiting for transfers between devices: 141 us -> 0 us
  blocking collectives: 137 us -> 0 us
  Pallas kernels: 0 us -> 87.7 us
  matrix products: 29.8 us -> 0 us
  local copies, waits for them, and re-layouts: 40.4 us -> 10.8 us
  other arithmetic: 16.1 us -> 2.58 us
  between operations: 14.4 us -> 0.91 us
    reduce_scatter x6 -> x0, waiting for transfers between devices: 141 us -> none  [the longest x2 73 us: to_modes(): lax.psum_scatter(jnp.einsum('kx,bdnxc->kbdnc', table_rows, section_y, pre...]
    all_gather x6 -> x0, blocking collectives: 97 us -> none  [the longest x2 63.1 us: from_modes(): lax.all_gather(hat_back, 'gz', axis=0, tiled=True)]
    pallas_call x0 -> x2, Pallas kernels: none -> 87.7 us  [call(): pl.pallas_call(functools.partial(layer_kernel, cfg), out_shape=list(outs....]
    psum x1 -> x0, blocking collectives: 40.3 us -> none  [point_total(): return lax.psum(point_term, ('gz', 'gy', 'gx'))]
    dot_general x20 -> x0, matrix products: 29.8 us -> none  [the longest x2 8.27 us: layer_back(): jnp.einsum('ijkao,ijko->ijka', weights, hat_grad, precision=highest)]
    reshape x4 -> x0, local copies, waits for them, and re-layouts: 11.2 us -> none  [the longest x2 7.51 us: layer_back(): weights = spectral.reshape(hat_in.shape + (channels,)).astype(jnp.float32)]
    convert_element_type x5 -> x0, local copies, waits for them, and re-layouts: 11.1 us -> none  [the longest x1 3 us: on_device(): upstream = grad_output.reshape(shape_local).astype(jnp.float32)]
    mul x2 -> x0, local copies, waits for them, and re-layouts: 9.66 us -> none  [layer_back(): hat_in[..., :, None] * hat_grad[..., None, :]]
  transfers between devices with their start and end apart: 6 -> 0, of which waited for: 5 -> 0; matrix products, arithmetic and copies ran while one was open for 8% -> 0% of each run, Pallas kernels for 0% -> 0%
where the time goes in v1:
time: 102 us
  Pallas kernels  87.7 us (86%)
  local copies, waits for them, and re-layouts  10.8 us (11%)
  other arithmetic  2.58 us (3%)
    pallas_call x2, Pallas kernels, call(): pl.pallas_call(functools.partial(layer_kernel, cfg), out_shape=list(outs....  87.7 us
    unnamed x37, local copies, waits for them, and re-layouts  5.33 us
    squeeze x1, local copies, waits for them, and re-layouts, on_device(): lax.dynamic_index_in_dim(const(kz_all.reshape(nx, lanes, MZ * chan)), lax...  4.75 us
    convert_element_type x1, other arithmetic, on_device(): mid = value_one.astype(bf16)  2.09 us

profile of v1, /device:TPU:0, one launch (start us, length us, event | category | flops | bytes accessed | tf_op | source)
XLA Modules:
  0.0 102.0 jit_solution(665616616315540263)
XLA Ops:
  0.6 2.1 %fusion.10 = (bf16[128,2048]{1,0:T(8,128)(2,1)S(1)}, bf16[128,2048]{1,0:T(8,128)(2,1)S(1)}) fusion(bf16[8,16,2048]{2,1,0:T(8,128)(2,1)} %param.20, bf16[8,16,2048]{2,1,0:T(8,128)(2,1)} %param.21, bf16[8,16,2048]{2,1,0:T(8,128)(2,1)} %param.22), kind=kLoop, calls=%fused_computation.20 | loop fusion | flops 4718592 | bytes 2621440 | tf_op jit(solution)/shard_map/convert_element_type | solution.py:370
  2.7 0.0 copy-start
  2.7 0.0 copy-start.1
  2.7 0.0 copy-start.2
  2.8 0.0 copy-start.4
  2.8 0.0 copy-start.5
  2.8 0.0 copy-start.6
  2.8 0.0 copy-start.7
  2.8 0.0 copy-start.8
  2.8 0.0 copy-start.9
  2.8 0.0 copy-start.10
  2.8 0.0 copy-start.11
  2.9 0.0 copy-start.12
  2.9 0.0 copy-start.13
  2.9 4.7 %dynamic-slice_bitcast_fusion.refs_5_.refs_7_ = bf16[2048,1024]{1,0:T(8,128)(2,1)} fusion(bf16[2,2048,1024]{2,1,0:T(8,128)(2,1)} %constant.42.clone, s32[]{:T(128)S(6)} %select_n.4), kind=kLoop, calls=%fused_computation | loop fusion | bytes 8388612 | tf_op jit(solution)/shard_map/jit(dynamic_index_in_dim)/squeeze | solution.py:279
  7.6 0.0 copy-done
  7.6 0.0 copy-done.1
  7.6 0.0 copy-done.2
  7.6 0.0 copy-done.4
  7.7 0.0 copy-done.5
  7.7 0.0 copy-done.6
  7.7 0.0 copy-done.7
  7.7 0.0 copy-done.8
  7.7 0.0 copy-done.9
  7.7 0.0 copy-done.10
  7.7 0.0 copy-done.11
  7.7 0.0 copy-done.12
  7.7 0.0 copy-done.13
  7.7 0.0 copy-start.16
  7.8 0.0 copy-start.3
  7.8 0.0 copy-start.14
  7.8 45.9 %layer_two.1 = (f32[128,2048]{1,0:T(8,128)S(1)}, f32[128,4096]{1,0:T(8,128)}, f32[128,128]{1,0:T(8,128)S(1)}) custom-call(bf16[128,2048]{1,0:T(8,128)(2,1)S(1)} %get-tuple-element.20.refs_0_.refs_3_, bf16[128,2048]{1,0:T(8,128)(2,1)S(1)} %get-tuple-element.19.refs_1_, bf16[128,2048]{1,0:T(8,128)(2,1)S(1)} %bitcast.23, bf16[128,4096]{1,0:T(8,128)(2,1)S(1)} %bitcast.25, ...), custom_call_target="tpu_custom_call" | custom-call | tf_op jit(solution)/shard_map/layer_two/pallas_call | solution.py:351
  53.7 0.0 copy-done.16
  53.7 0.5 fusion.15.refs_0_
  54.2 0.0 copy-done.3
  54.2 0.0 copy-done.14
  54.2 41.8 %layer_one.1 = (bf16[128,2048]{1,0:T(8,128)(2,1)S(1)}, f32[128,4096]{1,0:T(8,128)}, f32[64,128]{1,0:T(8,128)S(1)}) custom-call(bf16[128,2048]{1,0:T(8,128)(2,1)S(1)} %fusion.15.refs_0_, bf16[128,2048]{1,0:T(8,128)(2,1)S(1)} %get-tuple-element.19.refs_1_, bf16[128,2048]{1,0:T(8,128)(2,1)S(1)} %bitcast.24, ...), custom_call_target="tpu_custom_call" | custom-call | tf_op jit(solution)/shard_map/layer_one/pallas_call | solution.py:351
  96.0 0.0 copy-start.15
  96.0 0.7 fusion.17
  96.7 0.8 copy.27
  97.5 3.1 %copy.28 = f32[2,8,8,4096]{3,2,1,0:T(8,128)} copy(f32[2,8,8,4096]{3,2,1,0:T(8,128)} %bitcast.29) | data formatting | bytes 4194304
  100.6 0.0 copy-done.15
  100.6 1.3 %copy.29 = f32[2,8,8,4096]{3,2,1,0:T(8,128)} copy(f32[2,8,8,4096]{3,2,1,0:T(8,128)S(1)} %bitcast.28) | data formatting | bytes 4194304
Async XLA Ops:
  2.7 4.9 %copy-start = (bf16[4096,64]{1,0:T(8,128)(2,1)S(1)}, bf16[4096,64]{1,0:T(8,128)(2,1)}, u32[]{:S(2)}) copy-start(bf16[4096,64]{1,0:T(8,128)(2,1)} %constant.51.clone.refs_14_.refs_16_) | copy-start | bytes 1572868
  2.7 4.9 %copy-start.1 = (bf16[8,16,2048]{2,1,0:T(8,128)(2,1)S(1)}, bf16[8,16,2048]{2,1,0:T(8,128)(2,1)}, u32[]{:S(2)}) copy-start(bf16[8,16,2048]{2,1,0:T(8,128)(2,1)} %param.19) | copy-start | bytes 1572868
  2.7 4.9 %copy-start.2 = (bf16[2,8,8,4096]{3,2,1,0:T(8,128)(2,1)S(1)}, bf16[2,8,8,4096]{3,2,1,0:T(8,128)(2,1)}, u32[]{:S(2)}) copy-start(bf16[2,8,8,4096]{3,2,1,0:T(8,128)(2,1)} %param.24) | copy-start | bytes 3145732
  2.8 4.9 %copy-start.4 = (f32[128,512]{1,0:T(8,128)S(1)}, f32[128,512]{1,0:T(8,128)}, u32[]{:S(2)}) copy-start(f32[128,512]{1,0:T(8,128)} %constant.48.clone.refs_11_.refs_13_) | copy-start | bytes 786436
  2.8 4.9 %copy-start.5 = (bf16[8,128,64]{2,1,0:T(8,128)(2,1)S(1)}, bf16[8,128,64]{2,1,0:T(8,128)(2,1)}, u32[]{:S(2)}) copy-start(bf16[8,128,64]{2,1,0:T(8,128)(2,1)} %constant.44.clone.refs_7_.refs_9_) | copy-start | bytes 393220
  2.8 4.9 %copy-start.6 = (bf16[512,128]{1,0:T(8,128)(2,1)S(1)}, bf16[512,128]{1,0:T(8,128)(2,1)}, u32[]{:S(2)}) copy-start(bf16[512,128]{1,0:T(8,128)(2,1)} %constant.49.clone.refs_12_.refs_14_) | copy-start | bytes 393220
  2.8 4.9 %copy-start.7 = (bf16[8,64,128]{2,1,0:T(8,128)(2,1)S(1)}, bf16[8,64,128]{2,1,0:T(8,128)(2,1)}, u32[]{:S(2)}) copy-start(bf16[8,64,128]{2,1,0:T(8,128)(2,1)} %constant.45.clone.refs_8_.refs_10_) | copy-start | bytes 393220
  2.8 4.9 %copy-start.8 = (bf16[256,64]{1,0:T(8,128)(2,1)S(1)}, bf16[256,64]{1,0:T(8,128)(2,1)}, u32[]{:S(2)}) copy-start(bf16[256,64]{1,0:T(8,128)(2,1)} %constant.52.clone.refs_15_.refs_17_) | copy-start | bytes 98308
  2.8 4.9 %copy-start.9 = (bf16[64,512]{1,0:T(8,128)(2,1)S(1)}, bf16[64,512]{1,0:T(8,128)(2,1)}, u32[]{:S(2)}) copy-start(bf16[64,512]{1,0:T(8,128)(2,1)} %constant.50.clone.refs_13_.refs_15_) | copy-start | bytes 196612
  2.8 4.9 %copy-start.10 = (bf16[2,128,128]{2,1,0:T(8,128)(2,1)S(1)}, bf16[2,128,128]{2,1,0:T(8,128)(2,1)}, u32[]{:S(2)}) copy-start(bf16[2,128,128]{2,1,0:T(8,128)(2,1)} %constant.46.clone.refs_9_.refs_11_) | copy-start | bytes 196612
  2.8 4.9 %copy-start.11 = (bf16[2,128,128]{2,1,0:T(8,128)(2,1)S(1)}, bf16[2,128,128]{2,1,0:T(8,128)(2,1)}, u32[]{:S(2)}) copy-start(bf16[2,128,128]{2,1,0:T(8,128)(2,1)} %constant.43.clone.refs_6_.refs_8_) | copy-start | bytes 196612
  2.9 4.9 %copy-start.12 = (bf16[128,16]{1,0:T(8,128)(2,1)S(1)}, bf16[128,16]{1,0:T(8,128)(2,1)}, u32[]{:S(2)}) copy-start(bf16[128,16]{1,0:T(8,128)(2,1)} %constant.47.clone.refs_10_.refs_12_) | copy-start | bytes 12292
  2.9 4.9 %copy-start.13 = (bf16[64,64]{1,0:T(8,128)(2,1)S(1)}, bf16[64,64]{1,0:T(8,128)(2,1)}, u32[]{:S(2)}) copy-start(bf16[64,64]{1,0:T(8,128)(2,1)} %refs_4_.1) | copy-start | bytes 24580
  7.7 45.9 %copy-start.16 = (bf16[8,16,2048]{2,1,0:T(8,128)(2,1)S(1)}, bf16[8,16,2048]{2,1,0:T(8,128)(2,1)}, u32[]{:S(2)}) copy-start(bf16[8,16,2048]{2,1,0:T(8,128)(2,1)} %param.20) | copy-start | bytes 1572868
  7.8 46.4 %copy-start.3 = (bf16[2,8,8,4096]{3,2,1,0:T(8,128)(2,1)S(1)}, bf16[2,8,8,4096]{3,2,1,0:T(8,128)(2,1)}, u32[]{:S(2)}) copy-start(bf16[2,8,8,4096]{3,2,1,0:T(8,128)(2,1)} %param.23) | copy-start | bytes 3145732
  7.8 46.4 %copy-start.14 = (bf16[64,64]{1,0:T(8,128)(2,1)S(1)}, bf16[64,64]{1,0:T(8,128)(2,1)}, u32[]{:S(2)}) copy-start(bf16[64,64]{1,0:T(8,128)(2,1)} %refs_6_.2) | copy-start | bytes 24580
  96.0 4.6 %copy-start.15 = (f32[128,4096]{1,0:T(8,128)S(1)}, f32[128,4096]{1,0:T(8,128)}, u32[]{:S(2)}) copy-start(f32[128,4096]{1,0:T(8,128)} %get-tuple-element.15) | copy-start | bytes 6291460

commit v2 on v1

--- a/solution.py
+++ b/solution.py
@@ -67,6 +67,7 @@
     names = cfg["names"]
     r = dict(zip(names, refs))
     kz, ay, ax, axt, ayt = r["kz"], r["ay"], r["ax"], r["axt"], r["ayt"]
+    half = blane // 2
     gz, gy, gx = lax.axis_index("gz"), lax.axis_index("gy"), lax.axis_index("gx")
 
     def wrap(v, n):
@@ -81,6 +82,19 @@
 
     def b_device(j):
         return (wrap(gz + j, nz), gy, gx)
+
+    width = kz.shape[1]
+    tile = 256
+    lanes = kz.shape[0]
+    loads = {}
+    for h in range(2):
+        for px in range(nx):
+            n = 2 * px + h
+            cols = slice(n * half, (n + 1) * half)
+            loads[n] = pltpu.make_async_copy(
+                r["kz_all"].at[gx, :, cols], kz.at[:, cols], r["kz_sem"].at[n]
+            )
+            loads[n].start()
 
     barrier = pltpu.get_barrier_semaphore()
     for j in range(1, n_a):
@@ -88,14 +102,12 @@
     for j in range(1, nz):
         pl.semaphore_signal(barrier, 1, device_id=b_device(j), device_id_type=pl.DeviceIdType.MESH)
 
-    width = kz.shape[1]
-    tile = 256
-    lanes = kz.shape[0]
     copies = []
 
-    def remote(src, dst, sem, j, dev):
+    def remote(src, dst, sem, j, dev, h=0):
         c = pltpu.make_async_remote_copy(
-            src_ref=src, dst_ref=dst, send_sem=r[sem + "_s"].at[j], recv_sem=r[sem + "_r"].at[j],
+            src_ref=src, dst_ref=dst,
+            send_sem=r[sem + "_s"].at[h, j], recv_sem=r[sem + "_r"].at[h, j],
             device_id=dev, device_id_type=pl.DeviceIdType.MESH,
         )
         c.start()
@@ -113,49 +125,68 @@
 
         lax.fori_loop(0, width // tile, body, 0)
 
-    def block(py, px):
+    def block(py, px, h=None):
+        size = blane if h is None else half
         return (
             pl.ds(pl.multiple_of(py * brow, brow), brow),
-            pl.ds(pl.multiple_of(px * blane, blane), blane),
+            pl.ds(pl.multiple_of(px * blane + (h or 0) * half, half), size),
         )
 
-    def start_a(t):
+    a_order = sorted(range(1, n_a), key=lambda j: (j % nx == 0, j))
+
+    def start_a(t, h):
         out = []
-        for j in range(1, n_a):
-            rows, cols = block(*a_peer(j))
+        for j in a_order:
+            rows, cols = block(*a_peer(j), h)
             out.append(
-                remote(r["y"].at[t, rows, cols], r["land_a"].at[t, j], "a%d" % t, j, a_device(j))
+                remote(
+                    r["y"].at[t, rows, cols], r["land_a"].at[t, h, j], "a%d" % t, j, a_device(j), h
+                )
             )
         return out
 
     def finish_a(t, cs):
-        rows, cols = block(gy, gx)
-        for c in cs:
-            c.wait_recv()
-        total = r["y"][t, rows, cols]
-        for j in range(1, n_a):
-            total = total + r["land_a"][t, j]
-        part = mm(ax[gz], total)
-        for s in range(nz):
-            r["p"][t, s] = part[s * mrow : (s + 1) * mrow, :]
         out = []
-        for j in range(1, nz):
-            dev = b_device(j)
-            out.append(remote(r["p"].at[t, dev[0]], r["land_b"].at[t, j], "b%d" % t, j, dev))
+        for h in range(2):
+            rows, cols = block(gy, gx, h)
+            for c in cs[h]:
+                c.wait_recv()
+            total = r["y"][t, rows, cols]
+            for j in range(1, n_a):
+                total = total + r["land_a"][t, h, j]
+            part = mm(ax[gz], total)
+            for s in range(nz):
+                r["p"][t, h, s] = part[s * mrow : (s + 1) * mrow, :]
+            for j in range(1, nz):
+                dev = b_device(j)
+                out.append(
+                    remote(r["p"].at[t, h, dev[0]], r["land_b"].at[t, h, j], "b%d" % t, j, dev, h)
+                )
         return out
 
     def finish_b(t, cs, scale):
         for c in cs:
             c.wait_recv()
-        total = r["p"][t, gz]
-        for j in range(1, nz):
-            total = total + r["land_b"][t, j]
+        parts = []
+        for h in range(2):
+            total = r["p"][t, h, gz]
+            for j in range(1, nz):
+                total = total + r["land_b"][t, h, j]
+            parts.append(total)
+        total = jnp.concatenate(parts, axis=1)
         spread = mm(r["rep"][...], total * scale) * r["mask"][...]
         return mm(spread, r["fold"][...])
 
-    analyse(r["dz"], 0)
-    pl.semaphore_wait(barrier, n_a + nz - 2)
-    wait_a = start_a(0)
+    wait_a = []
+    for h in range(2):
+        for px in range(nx):
+            n = 2 * px + h
+            cols = slice(n * half, (n + 1) * half)
+            loads[n].wait()
+            r["y"][0, :, cols] = mm(ay[gy], mm(r["dz"][...], kz[:, cols]))
+        if h == 0:
+            pl.semaphore_wait(barrier, n_a + nz - 2)
+        wait_a.append(start_a(0, h))
     if first:
         lane = lax.broadcasted_iota(jnp.int32, (chan, 2 * chan), 1)
 
@@ -182,9 +213,9 @@
         ]
     else:
         analyse(r["mid"], 1)
-        wait_a1 = start_a(1)
+        wait_a1 = [start_a(1, 0), start_a(1, 1)]
         analyse(r["gin"], 2)
-        wait_a2 = start_a(2)
+        wait_a2 = [start_a(2, 0), start_a(2, 1)]
     wait_b = finish_a(0, wait_a)
     tall = mm_t(r["eye"][...], r["point"][...])
     square = mm_t(tall, r["eye"][...])
@@ -210,32 +241,35 @@
         w = r["weights"][:, n * 512 : (n + 1) * 512].astype(f32)
         back = back + mm(w * prod_tile, r["sum_o"][n * 512 : (n + 1) * 512, :])
     spread = mm(back, r["spread"][...]) * r["mask"][...]
-    r["c"][gz] = tmm(r["rep"][...], spread)
-    wait_c = [
-        remote(r["c"].at[gz], r["c"].at[gz], "c", j, b_device(j)) for j in range(1, nz)
-    ]
+    mixed = tmm(r["rep"][...], spread)
+    wait_c = []
+    for h in range(2):
+        r["c"][h, gz] = mixed[:, h * half : (h + 1) * half]
+        wait_c.append(
+            [
+                remote(r["c"].at[h, gz], r["c"].at[h, gz], "c", j, b_device(j), h)
+                for j in range(1, nz)
+            ]
+        )
     if not first:
         wait_b1 = finish_a(1, wait_a1)
         wait_b2 = finish_a(2, wait_a2)
-    for c in wait_c:
-        c.wait_recv()
-    for s in range(nz):
-        r["cat"][s * mrow : (s + 1) * mrow, :] = r["c"][s]
-    rows, cols = block(gy, gx)
-    r["v"][rows, cols] = mm(axt[gz], r["cat"][...])
-    wait_d = [
-        remote(r["v"].at[rows, cols], r["v"].at[rows, cols], "d", j, a_device(j))
-        for j in range(1, n_a)
-    ]
-    if first:
-        hat_in = r["hat_in"][...]
-    else:
-        hat_in = finish_b(1, wait_b1, a_scale)
-        r["hat_out"][...] = finish_b(2, wait_b2, a_scale)
-    low_in = hat_in[:, :chan]
-    for n in range(wide // 512):
-        cs = slice(n * 512, (n + 1) * 512)
-        r["spec"][:, cs] = mm_t(low_in, r["sum_o"][cs, :]) * prod_tile
+    wait_d = []
+    for h in range(2):
+        for c in wait_c[h]:
+            c.wait_recv()
+        for s in range(nz):
+            r["cat"][s * mrow : (s + 1) * mrow, :] = r["c"][h, s]
+        rows, cols = block(gy, gx, h)
+        r["v"][rows, cols] = mm(axt[gz], r["cat"][...])
+        wait_d += [
+            remote(r["v"].at[rows, cols], r["v"].at[rows, cols], "d", j, a_device(j), h)
+            for j in a_order
+        ]
+    r["hat"][...] = hat
+    if not first:
+        r["hat_in_two"][...] = finish_b(1, wait_b1, a_scale)
+        r["hat_in_one"][...] = finish_b(2, wait_b2, a_scale)
     if first:
         for c in wait_pb:
             c.wait_recv()
@@ -257,6 +291,12 @@
     lax.fori_loop(0, lanes // tile, body, 0)
     for c in copies:
         c.wait_send()
+
+
+def outer_kernel(chan, in_one, dz_one, in_two, dz_two, sum_o, spec_one, spec_two):
+    for hat_in, hat, out in ((in_one, dz_one, spec_one), (in_two, dz_two, spec_two)):
+        times = out.shape[1] // hat.shape[1]
+        out[...] = mm_t(hat_in[:, :chan], sum_o[...]) * jnp.concatenate([hat[...]] * times, axis=1)
 
 
 def on_device(
@@ -276,9 +316,7 @@
     kz_all = np.zeros((nx, cz, chan, MZ, chan), ml_dtypes.bfloat16)
     diag = np.arange(chan)
     kz_all[:, :, diag, :, diag] = tz.transpose(0, 2, 1).astype(ml_dtypes.bfloat16)[None]
-    kz = lax.dynamic_index_in_dim(
-        const(kz_all.reshape(nx, lanes, MZ * chan)), lax.axis_index("gx"), 0, False
-    )
+    kz_all = const(kz_all.reshape(nx, lanes, MZ * chan))
     ay = np.einsum("dky,xw->dkxwy", ty, np.eye(cx)).reshape(ny, MY * cx, cx * cy)
     ax = np.einsum("dkx,ab->dkabx", tx, np.eye(qy)).reshape(nz, MX * qy, qy * cx)
     modes = qx * qy * qz
@@ -292,7 +330,7 @@
     sum_o = np.repeat(eye, chan, axis=0)
     eye4 = np.tile(eye, (256 // chan, 1))
     tables = {
-        "kz": kz,
+        "kz_all": kz_all,
         "ay": const(ay),
         "ax": const(ax),
         "axt": const(ax.transpose(0, 2, 1)),
@@ -313,21 +351,24 @@
         t = 1 if first else 3
         outs = {
             "down": jax.ShapeDtypeStruct((rows, lanes), bf16 if first else f32),
-            "spec": jax.ShapeDtypeStruct((modes, chan * chan), f32),
+            "hat": jax.ShapeDtypeStruct((modes, 2 * chan), f32),
         }
         if first:
             outs["pt"] = jax.ShapeDtypeStruct((chan, 2 * chan), f32)
         else:
-            outs["hat_out"] = jax.ShapeDtypeStruct((modes, 2 * chan), f32)
+            outs["hat_in_one"] = jax.ShapeDtypeStruct((modes, 2 * chan), f32)
+            outs["hat_in_two"] = jax.ShapeDtypeStruct((modes, 2 * chan), f32)
         scratch = {
             "y": pltpu.VMEM((t, MY * cx, MZ * chan), f32),
-            "land_a": pltpu.VMEM((t, n_a, brow, blane), f32),
-            "p": pltpu.VMEM((t, nz, mrow, blane), f32),
-            "land_b": pltpu.VMEM((t, nz, mrow, blane), f32),
-            "c": pltpu.VMEM((nz, mrow, blane), f32),
-            "cat": pltpu.VMEM((nz * mrow, blane), f32),
+            "land_a": pltpu.VMEM((t, 2, n_a, brow, blane // 2), f32),
+            "p": pltpu.VMEM((t, 2, nz, mrow, blane // 2), f32),
+            "land_b": pltpu.VMEM((t, 2, nz, mrow, blane // 2), f32),
+            "c": pltpu.VMEM((2, nz, mrow, blane // 2), f32),
+            "cat": pltpu.VMEM((nz * mrow, blane // 2), f32),
             "v": pltpu.VMEM((MY * cx, MZ * chan), f32),
             "v2": pltpu.VMEM((rows, MZ * chan), bf16),
+            "kz": pltpu.VMEM((lanes, MZ * chan), bf16),
+            "kz_sem": pltpu.SemaphoreType.DMA((2 * nx,)),
             "p4": pltpu.VMEM((256, 256), bf16),
         }
         sems = {"c": nz, "d": n_a}
@@ -340,8 +381,8 @@
             sems["pa"] = n_a
             sems["pb"] = nz
         for k, n in sems.items():
-            scratch[k + "_s"] = pltpu.SemaphoreType.DMA((n,))
-            scratch[k + "_r"] = pltpu.SemaphoreType.DMA((n,))
+            scratch[k + "_s"] = pltpu.SemaphoreType.DMA((2, n))
+            scratch[k + "_r"] = pltpu.SemaphoreType.DMA((2, n))
         cfg = dict(
             nz=nz, ny=ny, nx=nx, first=first, brow=brow, blane=blane, mrow=mrow,
             scales=(a_scale, b_scale), chan=chan,
@@ -351,7 +392,9 @@
         got = pl.pallas_call(
             functools.partial(layer_kernel, cfg),
             out_shape=list(outs.values()),
-            in_specs=[vmem] * len(args),
+            in_specs=[
+                pl.BlockSpec(memory_space=pltpu.HBM) if k == "kz_all" else vmem for k in args
+            ],
             out_specs=[vmem] * len(outs),
             scratch_shapes=list(scratch.values()),
             compiler_params=pltpu.CompilerParams(
@@ -387,15 +430,25 @@
             "mid": mid,
             "gin": gin,
             "dz_two": dz_two,
-            "hat_in": two["hat_out"],
             "weights": spectral_one.reshape(modes, chan * chan),
             "point": point_one,
         },
     )
+    step = 1024
+    small = pl.BlockSpec((modes, 2 * chan), lambda n: (0, 0))
+    large = pl.BlockSpec((modes, step), lambda n: (0, n))
+    spec_one, spec_two = pl.pallas_call(
+        functools.partial(outer_kernel, chan),
+        grid=(chan * chan // step,),
+        out_shape=[jax.ShapeDtypeStruct((modes, chan * chan), f32)] * 2,
+        in_specs=[small] * 4 + [pl.BlockSpec((step, chan), lambda n: (n, 0))],
+        out_specs=[large] * 2,
+        name="outer",
+    )(two["hat_in_one"], one["hat"], two["hat_in_two"], two["hat"], tables["sum_o"])
     return (
         one["down"].reshape(grid_input.shape),
-        one["spec"].reshape(spectral_one.shape),
-        two["spec"].reshape(spectral_two.shape),
+        spec_one.reshape(spectral_one.shape),
+        spec_two.reshape(spectral_two.shape),
         one["pt"][:, chan:],
         one["pt"][:, :chan],
     )

time: 102 us -> 103 us (level)
  Pallas kernels: 87.7 us -> 85.3 us
  local copies, waits for them, and re-layouts: 10.8 us -> 13.2 us
    unnamed x37 -> x45, local copies, waits for them, and re-layouts: 5.33 us -> 12.5 us
    pallas_call x2, Pallas kernels: 87.7 us -> 80.9 us  [call(): pl.pallas_call(functools.partial(layer_kernel, cfg), out_shape=list(outs....]
    squeeze x1 -> x0, local copies, waits for them, and re-layouts: 4.75 us -> none  [on_device(): lax.dynamic_index_in_dim(const(kz_all.reshape(nx, lanes, MZ * chan)), lax...]
    pallas_call x0 -> x1, Pallas kernels: none -> 4.38 us  [on_device(): pl.pallas_call(functools.partial(outer_kernel, chan), grid=(chan * chan /...]
where the time goes in v2:
time: 103 us; the launch traced here: 102 us
  Pallas kernels  85.3 us (83%)
  local copies, waits for them, and re-layouts  13.2 us (13%)
  other arithmetic  2.73 us (3%)
    pallas_call x2, Pallas kernels, call(): pl.pallas_call(functools.partial(layer_kernel, cfg), out_shape=list(outs....  80.9 us
    unnamed x45, local copies, waits for them, and re-layouts  12.5 us
    pallas_call x1, Pallas kernels, on_device(): pl.pallas_call(functools.partial(outer_kernel, chan), grid=(chan * chan /...  4.38 us
    convert_element_type x1, other arithmetic, on_device(): mid = value_one.astype(bf16)  2.24 us

profile of v2, /device:TPU:0, one launch (start us, length us, event | category | flops | bytes accessed | tf_op | source)
XLA Modules:
  0.0 102.1 jit_solution(10254009504808669773)
XLA Ops:
  0.6 0.0 copy-start
  0.6 0.0 copy-start.1
  0.7 0.0 copy-start.2
  0.7 2.2 %fusion.10 = (bf16[128,2048]{1,0:T(8,128)(2,1)S(1)}, bf16[128,2048]{1,0:T(8,128)(2,1)S(1)}) fusion(bf16[8,16,2048]{2,1,0:T(8,128)(2,1)} %param.20, bf16[8,16,2048]{2,1,0:T(8,128)(2,1)} %param.21, bf16[8,16,2048]{2,1,0:T(8,128)(2,1)} %param.22), kind=kLoop, calls=%fused_computation.19 | loop fusion | flops 4718592 | bytes 2621440 | tf_op jit(solution)/shard_map/convert_element_type | solution.py:413
  2.9 0.0 copy-done
  2.9 0.0 copy-done.1
  2.9 0.0 copy-done.2
  2.9 0.0 copy-start.4
  2.9 0.9 copy-done.4
  3.9 0.0 copy-start.5
  3.9 0.9 copy-done.5
  4.8 0.0 copy-start.6
  4.8 0.9 copy-done.6
  5.7 0.0 copy-start.7
  5.7 0.9 copy-done.7
  6.6 0.0 copy-start.8
  6.6 0.8 copy-done.8
  7.5 0.0 copy-start.9
  7.5 0.8 copy-done.9
  8.3 0.0 copy-start.10
  8.3 0.8 copy-done.10
  9.2 0.0 copy-start.12
  9.2 0.8 copy-done.12
  10.0 0.0 copy-start.14
  10.0 0.8 copy-done.14
  10.8 0.0 copy-start.19
  10.8 0.7 copy-done.19
  11.5 0.0 copy-start.21
  11.5 43.6 %layer_two.1 = (f32[128,2048]{1,0:T(8,128)S(1)}, f32[128,128]{1,0:T(8,128)S(1)}, f32[128,128]{1,0:T(8,128)S(1)}, f32[128,128]{1,0:T(8,128)S(1)}) custom-call(bf16[128,2048]{1,0:T(8,128)(2,1)S(1)} %get-tuple-element.26.refs_0_.refs_3_, bf16[128,2048]{1,0:T(8,128)(2,1)S(1)} %get-tuple-element.25.refs_1_, bf16[128,2048]{1,0:T(8,128)(2,1)S(1)} %bitcast.21, ...), custom_call_target="tpu_custom_call" | custom-call | tf_op jit(solution)/shard_map/layer_two/pallas_call | solution.py:392
  55.1 0.0 copy-start.15
  55.1 0.6 copy-done.15
  55.7 0.0 copy-start.16
  55.7 0.6 copy-done.16
  56.3 0.0 copy-start.17
  56.3 0.6 copy-done.17
  57.0 0.0 copy-start.3
  57.0 0.0 copy-done.21
  57.0 0.5 fusion.15.refs_0_
  57.5 0.7 copy-done.3
  58.2 0.0 copy-done.11
  58.2 0.0 copy-done.13
  58.2 0.0 copy-done.20
  58.2 37.3 %layer_one.1 = (bf16[128,2048]{1,0:T(8,128)(2,1)S(1)}, f32[128,128]{1,0:T(8,128)S(1)}, f32[64,128]{1,0:T(8,128)S(1)}) custom-call(bf16[128,2048]{1,0:T(8,128)(2,1)S(1)} %fusion.15.refs_0_, bf16[128,2048]{1,0:T(8,128)(2,1)S(1)} %get-tuple-element.25.refs_1_, bf16[128,2048]{1,0:T(8,128)(2,1)S(1)} %bitcast.22, ...), custom_call_target="tpu_custom_call" | custom-call | tf_op jit(solution)/shard_map/layer_one/pallas_call | solution.py:392
  95.6 0.0 copy-start.18
  95.6 0.6 copy-done.18
  96.2 4.4 %outer.1 = (f32[128,4096]{1,0:T(8,128)}, f32[128,4096]{1,0:T(8,128)}) custom-call(f32[128,128]{1,0:T(8,128)} %copy-done.16, f32[128,128]{1,0:T(8,128)} %copy-done.18, f32[128,128]{1,0:T(8,128)} %copy-done.17, f32[128,128]{1,0:T(8,128)} %copy-done.15, bf16[4096,64]{1,0:T(8,128)(2,1)} %constant.41.clone.refs_14_.refs_15_.sum_o), custom_call_target="tpu_custom_call" | custom-call | tf_op jit(solution)/shard_map/outer/pallas_call | solution.py:440
  100.6 0.7 fusion.17
  101.3 0.8 copy.25
  (3 shorter events, 0.0 us)
Async XLA Ops:
  0.6 2.3 %copy-start = (bf16[4096,64]{1,0:T(8,128)(2,1)S(1)}, bf16[4096,64]{1,0:T(8,128)(2,1)}, u32[]{:S(2)}) copy-start(bf16[4096,64]{1,0:T(8,128)(2,1)} %constant.41.clone.refs_14_.refs_15_.sum_o) | copy-start | bytes 1572868
  0.6 2.3 %copy-start.1 = (bf16[8,16,2048]{2,1,0:T(8,128)(2,1)S(1)}, bf16[8,16,2048]{2,1,0:T(8,128)(2,1)}, u32[]{:S(2)}) copy-start(bf16[8,16,2048]{2,1,0:T(8,128)(2,1)} %param.19) | copy-start | bytes 1572868
  0.7 2.3 %copy-start.2 = (bf16[2,8,8,4096]{3,2,1,0:T(8,128)(2,1)S(1)}, bf16[2,8,8,4096]{3,2,1,0:T(8,128)(2,1)}, u32[]{:S(2)}) copy-start(bf16[2,8,8,4096]{3,2,1,0:T(8,128)(2,1)} %param.24) | copy-start | bytes 3145732
  2.9 1.0 copy-start.4
  3.9 0.9 copy-start.5
  4.8 0.9 copy-start.6
  5.7 0.9 copy-start.7
  6.6 0.8 copy-start.8
  7.5 0.8 copy-start.9
  8.3 0.8 copy-start.10
  9.2 0.8 copy-start.12
  10.0 0.8 copy-start.14
  10.8 0.7 copy-start.19
  11.5 45.5 %copy-start.21 = (bf16[8,16,2048]{2,1,0:T(8,128)(2,1)S(1)}, bf16[8,16,2048]{2,1,0:T(8,128)(2,1)}, u32[]{:S(2)}) copy-start(bf16[8,16,2048]{2,1,0:T(8,128)(2,1)} %param.20) | copy-start | bytes 1572868
  55.1 0.6 copy-start.15
  55.7 0.6 copy-start.16
  56.3 0.6 copy-start.17
  57.0 1.2 %copy-start.3 = (bf16[2,8,8,4096]{3,2,1,0:T(8,128)(2,1)S(1)}, bf16[2,8,8,4096]{3,2,1,0:T(8,128)(2,1)}, u32[]{:S(2)}) copy-start(bf16[2,8,8,4096]{3,2,1,0:T(8,128)(2,1)} %param.23) | copy-start | bytes 3145732
  57.0 1.2 %copy-start.11 = (bf16[64,512]{1,0:T(8,128)(2,1)S(1)}, bf16[64,512]{1,0:T(8,128)(2,1)}, u32[]{:S(2)}) copy-start(bf16[64,512]{1,0:T(8,128)(2,1)} %constant.40.clone.refs_13_.refs_14_) | copy-start | bytes 196612
  57.0 1.2 %copy-start.13 = (bf16[256,64]{1,0:T(8,128)(2,1)S(1)}, bf16[256,64]{1,0:T(8,128)(2,1)}, u32[]{:S(2)}) copy-start(bf16[256,64]{1,0:T(8,128)(2,1)} %constant.42.clone.refs_15_.refs_16_) | copy-start | bytes 98308
  57.0 1.2 %copy-start.20 = (bf16[64,64]{1,0:T(8,128)(2,1)S(1)}, bf16[64,64]{1,0:T(8,128)(2,1)}, u32[]{:S(2)}) copy-start(bf16[64,64]{1,0:T(8,128)(2,1)} %refs_5_.2) | copy-start | bytes 24580
  95.6 0.6 copy-start.18

commit v3 on v2

--- a/solution.py
+++ b/solution.py
@@ -66,7 +66,18 @@
     n_a = ny * nx
     names = cfg["names"]
     r = dict(zip(names, refs))
-    kz, ay, ax, axt, ayt = r["kz"], r["ay"], r["ax"], r["axt"], r["ayt"]
+    kz = r["kz"]
+
+    def table(name, index=None):
+        start, (count, rows, cols) = cfg["places"][name]
+        if index is None:
+            return r["pack"][start : start + rows, :cols]
+        return r["pack"][pl.ds(pl.multiple_of(start + index * rows, 16), rows), :cols]
+
+    modes = mrow * blane // chan
+    mask = lax.rem(
+        lax.broadcasted_iota(jnp.int32, (modes, blane), 0), blane // chan
+    ) == lax.div(lax.broadcasted_iota(jnp.int32, (modes, blane), 1), chan)
     half = blane // 2
     gz, gy, gx = lax.axis_index("gz"), lax.axis_index("gy"), lax.axis_index("gx")
 
@@ -115,7 +126,7 @@
         return c
 
     def analyse(src, t):
-        table_y = ay[gy]
+        table_y = table("ay", gy)
 
         def body(n, carry):
             cols = pl.ds(pl.multiple_of(n * tile, tile), tile)
@@ -154,7 +165,7 @@
             total = r["y"][t, rows, cols]
             for j in range(1, n_a):
                 total = total + r["land_a"][t, h, j]
-            part = mm(ax[gz], total)
+            part = mm(table("ax", gz), total)
             for s in range(nz):
                 r["p"][t, h, s] = part[s * mrow : (s + 1) * mrow, :]
             for j in range(1, nz):
@@ -174,8 +185,8 @@
                 total = total + r["land_b"][t, h, j]
             parts.append(total)
         total = jnp.concatenate(parts, axis=1)
-        spread = mm(r["rep"][...], total * scale) * r["mask"][...]
-        return mm(spread, r["fold"][...])
+        spread = jnp.where(mask, mm(table("rep"), total * scale), 0.0)
+        return mm(spread, table("fold"))
 
     wait_a = []
     for h in range(2):
@@ -183,7 +194,7 @@
             n = 2 * px + h
             cols = slice(n * half, (n + 1) * half)
             loads[n].wait()
-            r["y"][0, :, cols] = mm(ay[gy], mm(r["dz"][...], kz[:, cols]))
+            r["y"][0, :, cols] = mm(table("ay", gy), mm(r["dz"][...], kz[:, cols]))
         if h == 0:
             pl.semaphore_wait(barrier, n_a + nz - 2)
         wait_a.append(start_a(0, h))
@@ -217,8 +228,8 @@
         analyse(r["gin"], 2)
         wait_a2 = [start_a(2, 0), start_a(2, 1)]
     wait_b = finish_a(0, wait_a)
-    tall = mm_t(r["eye"][...], r["point"][...])
-    square = mm_t(tall, r["eye"][...])
+    tall = mm_t(table("eye"), r["point"][...])
+    square = mm_t(tall, table("eye"))
     row_i = lax.broadcasted_iota(jnp.int32, square.shape, 0) // chan
     col_i = lax.broadcasted_iota(jnp.int32, square.shape, 1) // chan
     r["p4"][...] = jnp.where(row_i == col_i, square, 0.0).astype(bf16)
@@ -240,8 +251,8 @@
     for n in range(wide // 512):
         w = r["weights"][:, n * 512 : (n + 1) * 512].astype(f32)
         back = back + mm(w * prod_tile, r["sum_o"][n * 512 : (n + 1) * 512, :])
-    spread = mm(back, r["spread"][...]) * r["mask"][...]
-    mixed = tmm(r["rep"][...], spread)
+    spread = jnp.where(mask, mm_t(back, table("fold")[:, :chan]), 0.0)
+    mixed = tmm(table("rep"), spread)
     wait_c = []
     for h in range(2):
         r["c"][h, gz] = mixed[:, h * half : (h + 1) * half]
@@ -261,15 +272,15 @@
         for s in range(nz):
             r["cat"][s * mrow : (s + 1) * mrow, :] = r["c"][h, s]
         rows, cols = block(gy, gx, h)
-        r["v"][rows, cols] = mm(axt[gz], r["cat"][...])
+        r["v"][rows, cols] = mm(table("axt", gz), r["cat"][...])
         wait_d += [
             remote(r["v"].at[rows, cols], r["v"].at[rows, cols], "d", j, a_device(j), h)
             for j in a_order
         ]
-    r["hat"][...] = hat
+    r["hat"][0] = hat
     if not first:
-        r["hat_in_two"][...] = finish_b(1, wait_b1, a_scale)
-        r["hat_in_one"][...] = finish_b(2, wait_b2, a_scale)
+        r["hat"][1] = finish_b(1, wait_b1, a_scale)
+        r["hat"][2] = finish_b(2, wait_b2, a_scale)
     if first:
         for c in wait_pb:
             c.wait_recv()
@@ -279,7 +290,7 @@
         r["pt"][...] = total * b_scale
     for c in wait_d:
         c.wait_recv()
-    r["v2"][...] = (mm(ayt[gy], r["v"][...]) * a_scale).astype(bf16)
+    r["v2"][...] = (mm(table("ayt", gy), r["v"][...]) * a_scale).astype(bf16)
 
     def body(n, carry):
         cs = pl.ds(pl.multiple_of(n * tile, tile), tile)
@@ -293,10 +304,13 @@
         c.wait_send()
 
 
-def outer_kernel(chan, in_one, dz_one, in_two, dz_two, sum_o, spec_one, spec_two):
-    for hat_in, hat, out in ((in_one, dz_one, spec_one), (in_two, dz_two, spec_two)):
+def outer_kernel(chan, hat_one, hat_two, sum_o, spec_one, spec_two):
+    for hat_in, hat, out in (
+        (hat_two[2], hat_one[0], spec_one),
+        (hat_two[1], hat_two[0], spec_two),
+    ):
         times = out.shape[1] // hat.shape[1]
-        out[...] = mm_t(hat_in[:, :chan], sum_o[...]) * jnp.concatenate([hat[...]] * times, axis=1)
+        out[...] = mm_t(hat_in[:, :chan], sum_o[...]) * jnp.concatenate([hat] * times, axis=1)
 
 
 def on_device(
@@ -324,23 +338,30 @@
     blane = qz * chan
     mode = np.arange(modes)
     rep = (mode[:, None] // qz == np.arange(mrow)[None, :]).astype(np.float32)
-    mask = (mode[:, None] % qz == np.arange(blane)[None, :] // chan).astype(np.float32)
     fold = np.tile(np.concatenate([eye, eye], axis=1), (qz, 1))
-    spread = np.tile(eye, (1, qz))
     sum_o = np.repeat(eye, chan, axis=0)
     eye4 = np.tile(eye, (256 // chan, 1))
+    pieces = {
+        "ay": ay,
+        "ax": ax,
+        "axt": ax.transpose(0, 2, 1),
+        "ayt": ay.transpose(0, 2, 1),
+        "rep": rep[None],
+        "fold": fold[None],
+        "eye": eye4[None],
+    }
+    places, packed, start = {}, [], 0
+    pack_cols = max(v.shape[2] for v in pieces.values())
+    for k, v in pieces.items():
+        assert v.shape[1] % 16 == 0
+        places[k] = (start, v.shape)
+        start += v.shape[0] * v.shape[1]
+        flat_rows = v.reshape(-1, v.shape[2])
+        packed.append(np.pad(flat_rows, ((0, 0), (0, pack_cols - v.shape[2]))))
     tables = {
         "kz_all": kz_all,
-        "ay": const(ay),
-        "ax": const(ax),
-        "axt": const(ax.transpose(0, 2, 1)),
-        "ayt": const(ay.transpose(0, 2, 1)),
-        "rep": const(rep),
-        "mask": jnp.asarray(mask),
-        "fold": const(fold),
-        "spread": const(spread),
+        "pack": const(np.concatenate(packed)),
         "sum_o": const(sum_o),
-        "eye": const(eye4),
     }
     rows = cx * cy
     brow = qy * cx
@@ -351,13 +372,10 @@
         t = 1 if first else 3
         outs = {
             "down": jax.ShapeDtypeStruct((rows, lanes), bf16 if first else f32),
-            "hat": jax.ShapeDtypeStruct((modes, 2 * chan), f32),
+            "hat": jax.ShapeDtypeStruct((t, modes, 2 * chan), f32),
         }
         if first:
             outs["pt"] = jax.ShapeDtypeStruct((chan, 2 * chan), f32)
-        else:
-            outs["hat_in_one"] = jax.ShapeDtypeStruct((modes, 2 * chan), f32)
-            outs["hat_in_two"] = jax.ShapeDtypeStruct((modes, 2 * chan), f32)
         scratch = {
             "y": pltpu.VMEM((t, MY * cx, MZ * chan), f32),
             "land_a": pltpu.VMEM((t, 2, n_a, brow, blane // 2), f32),
@@ -384,6 +402,7 @@
             scratch[k + "_s"] = pltpu.SemaphoreType.DMA((2, n))
             scratch[k + "_r"] = pltpu.SemaphoreType.DMA((2, n))
         cfg = dict(
+            places=places,
             nz=nz, ny=ny, nx=nx, first=first, brow=brow, blane=blane, mrow=mrow,
             scales=(a_scale, b_scale), chan=chan,
             names=list(args) + list(outs) + list(scratch),
@@ -393,7 +412,8 @@
             functools.partial(layer_kernel, cfg),
             out_shape=list(outs.values()),
             in_specs=[
-                pl.BlockSpec(memory_space=pltpu.HBM) if k == "kz_all" else vmem for k in args
+                pl.BlockSpec(memory_space=pltpu.HBM) if k == "kz_all" else vmem
+                for k in args
             ],
             out_specs=[vmem] * len(outs),
             scratch_shapes=list(scratch.values()),
@@ -435,16 +455,16 @@
         },
     )
     step = 1024
-    small = pl.BlockSpec((modes, 2 * chan), lambda n: (0, 0))
+    small = [pl.BlockSpec((t, modes, 2 * chan), lambda n: (0, 0, 0)) for t in (1, 3)]
     large = pl.BlockSpec((modes, step), lambda n: (0, n))
     spec_one, spec_two = pl.pallas_call(
         functools.partial(outer_kernel, chan),
         grid=(chan * chan // step,),
         out_shape=[jax.ShapeDtypeStruct((modes, chan * chan), f32)] * 2,
-        in_specs=[small] * 4 + [pl.BlockSpec((step, chan), lambda n: (n, 0))],
+        in_specs=small + [pl.BlockSpec((step, chan), lambda n: (n, 0))],
         out_specs=[large] * 2,
         name="outer",
-    )(two["hat_in_one"], one["hat"], two["hat_in_two"], two["hat"], tables["sum_o"])
+    )(one["hat"], two["hat"], tables["sum_o"])
     return (
         one["down"].reshape(grid_input.shape),
         spec_one.reshape(spectral_one.shape),

time: 103 us -> 93.9 us (0.912)
  local copies, waits for them, and re-layouts: 13.2 us -> 4.74 us
    unnamed x45 -> x21, local copies, waits for them, and re-layouts: 12.5 us -> 4.05 us
where the time goes in v3:
time: 93.9 us; the launch traced here: 93.5 us
  Pallas kernels  85.3 us (91%)
  local copies, waits for them, and re-layouts  4.74 us (5%)
  other arithmetic  2.73 us (3%)
    pallas_call x2, Pallas kernels, call(): pl.pallas_call(functools.partial(layer_kernel, cfg), out_shape=list(outs....  80.9 us
    pallas_call x1, Pallas kernels, on_device(): pl.pallas_call(functools.partial(outer_kernel, chan), grid=(chan * chan /...  4.4 us
    unnamed x21, local copies, waits for them, and re-layouts  4.05 us
    convert_element_type x1, other arithmetic, on_device(): mid = value_one.astype(bf16)  2.24 us

profile of v3, /device:TPU:0, one launch (start us, length us, event | category | flops | bytes accessed | tf_op | source)
XLA Modules:
  0.0 93.5 jit_solution(12784260898584781053)
XLA Ops:
  0.6 0.0 copy-start.1
  0.6 0.0 copy-start
  0.7 0.0 copy-start.2
  0.7 0.0 copy-start.7
  0.7 2.2 %fusion.10 = (bf16[128,2048]{1,0:T(8,128)(2,1)S(1)}, bf16[128,2048]{1,0:T(8,128)(2,1)S(1)}) fusion(bf16[8,16,2048]{2,1,0:T(8,128)(2,1)} %param.12, bf16[8,16,2048]{2,1,0:T(8,128)(2,1)} %param.13, bf16[8,16,2048]{2,1,0:T(8,128)(2,1)} %param.14), kind=kLoop, calls=%fused_computation.19 | loop fusion | flops 4718592 | bytes 2621440 | tf_op jit(solution)/shard_map/convert_element_type | solution.py:433
  2.9 0.0 copy-done.1
  2.9 0.0 copy-done
  2.9 0.0 copy-done.2
  2.9 0.0 copy-done.7
  3.0 0.0 copy-start.3
  3.0 1.2 %copy-done.3 = bf16[2,8,8,4096]{3,2,1,0:T(8,128)(2,1)S(1)} copy-done((bf16[2,8,8,4096]{3,2,1,0:T(8,128)(2,1)S(1)}, bf16[2,8,8,4096]{3,2,1,0:T(8,128)(2,1)}, u32[]{:S(2)}) %copy-start.3) | copy-done | bytes 1048600
  4.2 0.0 copy-start.9
  4.2 43.6 %layer_two.1 = (f32[128,2048]{1,0:T(8,128)S(1)}, f32[3,128,128]{2,1,0:T(8,128)S(1)}) custom-call(bf16[128,2048]{1,0:T(8,128)(2,1)S(1)} %get-tuple-element.22.refs_0_.refs_3_, bf16[128,2048]{1,0:T(8,128)(2,1)S(1)} %get-tuple-element.21.refs_1_, bf16[128,2048]{1,0:T(8,128)(2,1)S(1)} %bitcast.21, bf16[128,4096]{1,0:T(8,128)(2,1)S(1)} %bitcast.23, ...), custom_call_target="tpu_custom_call" | custom-call | tf_op jit(solution)/shard_map/layer_two/pallas_call | solution.py:411
  47.8 0.0 copy-start.5
  47.8 0.7 copy-done.5
  48.5 0.0 copy-start.4
  48.5 0.0 copy-start.8
  48.5 0.0 copy-done.9
  48.5 0.5 fusion.15.refs_0_
  49.0 0.7 copy-done.4
  49.7 0.0 copy-done.8
  49.7 37.3 %layer_one.1 = (bf16[128,2048]{1,0:T(8,128)(2,1)S(1)}, f32[1,128,128]{2,1,0:T(8,128)S(1)}, f32[64,128]{1,0:T(8,128)S(1)}) custom-call(bf16[128,2048]{1,0:T(8,128)(2,1)S(1)} %fusion.15.refs_0_, bf16[128,2048]{1,0:T(8,128)(2,1)S(1)} %get-tuple-element.21.refs_1_, bf16[128,2048]{1,0:T(8,128)(2,1)S(1)} %bitcast.22, ...), custom_call_target="tpu_custom_call" | custom-call | tf_op jit(solution)/shard_map/layer_one/pallas_call | solution.py:411
  87.0 0.0 copy-start.6
  87.0 0.6 copy-done.6
  87.7 4.4 %outer.1 = (f32[128,4096]{1,0:T(8,128)}, f32[128,4096]{1,0:T(8,128)}) custom-call(f32[1,128,128]{2,1,0:T(8,128)} %copy-done.6, f32[3,128,128]{2,1,0:T(8,128)} %copy-done.5, bf16[4096,64]{1,0:T(8,128)(2,1)} %constant.18.clone.refs_7_.refs_8_.sum_o), custom_call_target="tpu_custom_call" | custom-call | tf_op jit(solution)/shard_map/outer/pallas_call | solution.py:460
  92.1 0.7 fusion.17
  92.7 0.8 copy.17
Async XLA Ops:
  0.6 2.3 %copy-start.1 = (bf16[2944,128]{1,0:T(8,128)(2,1)S(1)}, bf16[2944,128]{1,0:T(8,128)(2,1)}, u32[]{:S(2)}) copy-start(bf16[2944,128]{1,0:T(8,128)(2,1)} %constant.17.clone.refs_6_.refs_7_) | copy-start | bytes 2260996
  0.6 2.3 %copy-start = (bf16[4096,64]{1,0:T(8,128)(2,1)S(1)}, bf16[4096,64]{1,0:T(8,128)(2,1)}, u32[]{:S(2)}) copy-start(bf16[4096,64]{1,0:T(8,128)(2,1)} %constant.18.clone.refs_7_.refs_8_.sum_o) | copy-start | bytes 1572868
  0.7 2.3 %copy-start.2 = (bf16[8,16,2048]{2,1,0:T(8,128)(2,1)S(1)}, bf16[8,16,2048]{2,1,0:T(8,128)(2,1)}, u32[]{:S(2)}) copy-start(bf16[8,16,2048]{2,1,0:T(8,128)(2,1)} %param.11) | copy-start | bytes 1572868
  0.7 2.3 %copy-start.7 = (bf16[64,64]{1,0:T(8,128)(2,1)S(1)}, bf16[64,64]{1,0:T(8,128)(2,1)}, u32[]{:S(2)}) copy-start(bf16[64,64]{1,0:T(8,128)(2,1)} %refs_4_.1) | copy-start | bytes 24580
  3.0 1.2 %copy-start.3 = (bf16[2,8,8,4096]{3,2,1,0:T(8,128)(2,1)S(1)}, bf16[2,8,8,4096]{3,2,1,0:T(8,128)(2,1)}, u32[]{:S(2)}) copy-start(bf16[2,8,8,4096]{3,2,1,0:T(8,128)(2,1)} %param.16) | copy-start | bytes 3145732
  4.2 44.3 %copy-start.9 = (bf16[8,16,2048]{2,1,0:T(8,128)(2,1)S(1)}, bf16[8,16,2048]{2,1,0:T(8,128)(2,1)}, u32[]{:S(2)}) copy-start(bf16[8,16,2048]{2,1,0:T(8,128)(2,1)} %param.12) | copy-start | bytes 1572868
  47.8 0.7 copy-start.5
  48.5 1.2 %copy-start.4 = (bf16[2,8,8,4096]{3,2,1,0:T(8,128)(2,1)S(1)}, bf16[2,8,8,4096]{3,2,1,0:T(8,128)(2,1)}, u32[]{:S(2)}) copy-start(bf16[2,8,8,4096]{3,2,1,0:T(8,128)(2,1)} %param.15) | copy-start | bytes 3145732
  48.5 1.2 %copy-start.8 = (bf16[64,64]{1,0:T(8,128)(2,1)S(1)}, bf16[64,64]{1,0:T(8,128)(2,1)}, u32[]{:S(2)}) copy-start(bf16[64,64]{1,0:T(8,128)(2,1)} %refs_5_.2) | copy-start | bytes 24580
  87.0 0.6 copy-start.6

commit v4 on v3

--- a/solution.py
+++ b/solution.py
@@ -143,27 +143,40 @@
             pl.ds(pl.multiple_of(px * blane + (h or 0) * half, half), size),
         )
 
-    a_order = sorted(range(1, n_a), key=lambda j: (j % nx == 0, j))
-
     def start_a(t, h):
-        out = []
-        for j in a_order:
-            rows, cols = block(*a_peer(j), h)
-            out.append(
-                remote(
-                    r["y"].at[t, rows, cols], r["land_a"].at[t, h, j], "a%d" % t, j, a_device(j), h
+        out = {}
+        for dx in list(range(1, nx)) + [0]:
+            for dy in range(1, ny):
+                j = dy * nx + dx
+                rows, cols = block(*a_peer(j), h)
+                out[j] = remote(
+                    r["y"].at[t, rows, cols], r["land_a"].at[t, h, j], "a%d" % t, j,
+                    a_device(dy * nx), h,
                 )
-            )
         return out
+
+    def middle_a(t, cs):
+        for h in range(2):
+            for dx in range(1, nx):
+                rows, cols = block(*a_peer(dx), h)
+                total = r["y"][t, rows, cols]
+                for dy in range(1, ny):
+                    j = dy * nx + dx
+                    cs[h].pop(j).wait_recv()
+                    total = total + r["land_a"][t, h, j]
+                r["y"][t, rows, cols] = total
+                cs[h][dx] = remote(
+                    r["y"].at[t, rows, cols], r["land_a"].at[t, h, dx], "a%d" % t, dx,
+                    a_device(dx), h,
+                )
 
     def finish_a(t, cs):
         out = []
         for h in range(2):
             rows, cols = block(gy, gx, h)
-            for c in cs[h]:
+            total = r["y"][t, rows, cols]
+            for j, c in cs[h].items():
                 c.wait_recv()
-            total = r["y"][t, rows, cols]
-            for j in range(1, n_a):
                 total = total + r["land_a"][t, h, j]
             part = mm(table("ax", gz), total)
             for s in range(nz):
@@ -198,6 +211,7 @@
         if h == 0:
             pl.semaphore_wait(barrier, n_a + nz - 2)
         wait_a.append(start_a(0, h))
+    middle_a(0, wait_a)
     if first:
         lane = lax.broadcasted_iota(jnp.int32, (chan, 2 * chan), 1)
 
@@ -228,6 +242,9 @@
         analyse(r["gin"], 2)
         wait_a2 = [start_a(2, 0), start_a(2, 1)]
     wait_b = finish_a(0, wait_a)
+    if not first:
+        middle_a(1, wait_a1)
+        middle_a(2, wait_a2)
     tall = mm_t(table("eye"), r["point"][...])
     square = mm_t(tall, table("eye"))
     row_i = lax.broadcasted_iota(jnp.int32, square.shape, 0) // chan
@@ -273,10 +290,21 @@
             r["cat"][s * mrow : (s + 1) * mrow, :] = r["c"][h, s]
         rows, cols = block(gy, gx, h)
         r["v"][rows, cols] = mm(table("axt", gz), r["cat"][...])
-        wait_d += [
-            remote(r["v"].at[rows, cols], r["v"].at[rows, cols], "d", j, a_device(j), h)
-            for j in a_order
-        ]
+        direct = {}
+        for j in list(range(1, nx)) + [dy * nx for dy in range(1, ny)]:
+            direct[j] = remote(
+                r["v"].at[rows, cols], r["v"].at[rows, cols], "d", j, a_device(j), h
+            )
+        wait_d.append(direct)
+    for h in range(2):
+        for dx in range(1, nx):
+            wait_d[h].pop(dx).wait_recv()
+            rows, cols = block(gy, wrap(gx + nx - dx, nx), h)
+            for dy in range(1, ny):
+                j = dy * nx + dx
+                wait_d[h][j] = remote(
+                    r["v"].at[rows, cols], r["v"].at[rows, cols], "d", j, a_device(dy * nx), h
+                )
     r["hat"][0] = hat
     if not first:
         r["hat"][1] = finish_b(1, wait_b1, a_scale)
@@ -288,8 +316,9 @@
         for j in range(1, nz):
             total = total + r["pt_b"][j]
         r["pt"][...] = total * b_scale
-    for c in wait_d:
-        c.wait_recv()
+    for h in range(2):
+        for c in wait_d[h].values():
+            c.wait_recv()
     r["v2"][...] = (mm(table("ayt", gy), r["v"][...]) * a_scale).astype(bf16)
 
     def body(n, carry):

time: 93.9 us -> 95.4 us (1.016)
  Pallas kernels: 85.3 us -> 86.9 us
    pallas_call x2, Pallas kernels: 80.9 us -> 82.5 us  [call(): pl.pallas_call(functools.partial(layer_kernel, cfg), out_shape=list(outs....]
where the time goes in v4:
time: 95.4 us; the launch traced here: 95.1 us
  Pallas kernels  86.9 us (91%)
  local copies, waits for them, and re-layouts  4.74 us (5%)
  other arithmetic  2.73 us (3%)
    pallas_call x2, Pallas kernels, call(): pl.pallas_call(functools.partial(layer_kernel, cfg), out_shape=list(outs....  82.5 us
    pallas_call x1, Pallas kernels, on_device(): pl.pallas_call(functools.partial(outer_kernel, chan), grid=(chan * chan /...  4.4 us
    unnamed x21, local copies, waits for them, and re-layouts  4.05 us
    convert_element_type x1, other arithmetic, on_device(): mid = value_one.astype(bf16)  2.24 us

profile of v4, /device:TPU:0, one launch (start us, length us, event | category | flops | bytes accessed | tf_op | source)
XLA Modules:
  0.0 95.1 jit_solution(18080909330426972658)
XLA Ops:
  0.6 0.0 copy-start.1
  0.6 0.0 copy-start
  0.7 0.0 copy-start.2
  0.7 0.0 copy-start.7
  0.7 2.2 %fusion.10 = (bf16[128,2048]{1,0:T(8,128)(2,1)S(1)}, bf16[128,2048]{1,0:T(8,128)(2,1)S(1)}) fusion(bf16[8,16,2048]{2,1,0:T(8,128)(2,1)} %param.12, bf16[8,16,2048]{2,1,0:T(8,128)(2,1)} %param.13, bf16[8,16,2048]{2,1,0:T(8,128)(2,1)} %param.14), kind=kLoop, calls=%fused_computation.19 | loop fusion | flops 4718592 | bytes 2621440 | tf_op jit(solution)/shard_map/convert_element_type | solution.py:462
  2.9 0.0 copy-done.1
  2.9 0.0 copy-done
  2.9 0.0 copy-done.2
  2.9 0.0 copy-done.7
  3.0 0.0 copy-start.3
  3.0 1.2 %copy-done.3 = bf16[2,8,8,4096]{3,2,1,0:T(8,128)(2,1)S(1)} copy-done((bf16[2,8,8,4096]{3,2,1,0:T(8,128)(2,1)S(1)}, bf16[2,8,8,4096]{3,2,1,0:T(8,128)(2,1)}, u32[]{:S(2)}) %copy-start.3) | copy-done | bytes 1048600
  4.2 0.0 copy-start.9
  4.2 44.1 %layer_two.1 = (f32[128,2048]{1,0:T(8,128)S(1)}, f32[3,128,128]{2,1,0:T(8,128)S(1)}) custom-call(bf16[128,2048]{1,0:T(8,128)(2,1)S(1)} %get-tuple-element.22.refs_0_.refs_3_, bf16[128,2048]{1,0:T(8,128)(2,1)S(1)} %get-tuple-element.21.refs_1_, bf16[128,2048]{1,0:T(8,128)(2,1)S(1)} %bitcast.21, bf16[128,4096]{1,0:T(8,128)(2,1)S(1)} %bitcast.23, ...), custom_call_target="tpu_custom_call" | custom-call | tf_op jit(solution)/shard_map/layer_two/pallas_call | solution.py:440
  48.3 0.0 copy-start.5
  48.3 0.7 copy-done.5
  49.0 0.0 copy-start.4
  49.0 0.0 copy-start.8
  49.0 0.0 copy-done.9
  49.0 0.5 fusion.15.refs_0_
  49.5 0.7 copy-done.4
  50.2 0.0 copy-done.8
  50.2 38.4 %layer_one.1 = (bf16[128,2048]{1,0:T(8,128)(2,1)S(1)}, f32[1,128,128]{2,1,0:T(8,128)S(1)}, f32[64,128]{1,0:T(8,128)S(1)}) custom-call(bf16[128,2048]{1,0:T(8,128)(2,1)S(1)} %fusion.15.refs_0_, bf16[128,2048]{1,0:T(8,128)(2,1)S(1)} %get-tuple-element.21.refs_1_, bf16[128,2048]{1,0:T(8,128)(2,1)S(1)} %bitcast.22, ...), custom_call_target="tpu_custom_call" | custom-call | tf_op jit(solution)/shard_map/layer_one/pallas_call | solution.py:440
  88.6 0.0 copy-start.6
  88.6 0.6 copy-done.6
  89.3 4.4 %outer.1 = (f32[128,4096]{1,0:T(8,128)}, f32[128,4096]{1,0:T(8,128)}) custom-call(f32[1,128,128]{2,1,0:T(8,128)} %copy-done.6, f32[3,128,128]{2,1,0:T(8,128)} %copy-done.5, bf16[4096,64]{1,0:T(8,128)(2,1)} %constant.18.clone.refs_7_.refs_8_.sum_o), custom_call_target="tpu_custom_call" | custom-call | tf_op jit(solution)/shard_map/outer/pallas_call | solution.py:489
  93.7 0.7 fusion.17
  94.3 0.8 copy.17
Async XLA Ops:
  0.6 2.3 %copy-start.1 = (bf16[2944,128]{1,0:T(8,128)(2,1)S(1)}, bf16[2944,128]{1,0:T(8,128)(2,1)}, u32[]{:S(2)}) copy-start(bf16[2944,128]{1,0:T(8,128)(2,1)} %constant.17.clone.refs_6_.refs_7_) | copy-start | bytes 2260996
  0.6 2.3 %copy-start = (bf16[4096,64]{1,0:T(8,128)(2,1)S(1)}, bf16[4096,64]{1,0:T(8,128)(2,1)}, u32[]{:S(2)}) copy-start(bf16[4096,64]{1,0:T(8,128)(2,1)} %constant.18.clone.refs_7_.refs_8_.sum_o) | copy-start | bytes 1572868
  0.7 2.3 %copy-start.2 = (bf16[8,16,2048]{2,1,0:T(8,128)(2,1)S(1)}, bf16[8,16,2048]{2,1,0:T(8,128)(2,1)}, u32[]{:S(2)}) copy-start(bf16[8,16,2048]{2,1,0:T(8,128)(2,1)} %param.11) | copy-start | bytes 1572868
  0.7 2.3 %copy-start.7 = (bf16[64,64]{1,0:T(8,128)(2,1)S(1)}, bf16[64,64]{1,0:T(8,128)(2,1)}, u32[]{:S(2)}) copy-start(bf16[64,64]{1,0:T(8,128)(2,1)} %refs_4_.1) | copy-start | bytes 24580
  3.0 1.2 %copy-start.3 = (bf16[2,8,8,4096]{3,2,1,0:T(8,128)(2,1)S(1)}, bf16[2,8,8,4096]{3,2,1,0:T(8,128)(2,1)}, u32[]{:S(2)}) copy-start(bf16[2,8,8,4096]{3,2,1,0:T(8,128)(2,1)} %param.16) | copy-start | bytes 3145732
  4.2 44.8 %copy-start.9 = (bf16[8,16,2048]{2,1,0:T(8,128)(2,1)S(1)}, bf16[8,16,2048]{2,1,0:T(8,128)(2,1)}, u32[]{:S(2)}) copy-start(bf16[8,16,2048]{2,1,0:T(8,128)(2,1)} %param.12) | copy-start | bytes 1572868
  48.3 0.7 copy-start.5
  49.0 1.2 %copy-start.4 = (bf16[2,8,8,4096]{3,2,1,0:T(8,128)(2,1)S(1)}, bf16[2,8,8,4096]{3,2,1,0:T(8,128)(2,1)}, u32[]{:S(2)}) copy-start(bf16[2,8,8,4096]{3,2,1,0:T(8,128)(2,1)} %param.15) | copy-start | bytes 3145732
  49.0 1.2 %copy-start.8 = (bf16[64,64]{1,0:T(8,128)(2,1)S(1)}, bf16[64,64]{1,0:T(8,128)(2,1)}, u32[]{:S(2)}) copy-start(bf16[64,64]{1,0:T(8,128)(2,1)} %refs_5_.2) | copy-start | bytes 24580
  88.6 0.6 copy-start.6
